TPU v7x, 32 devices: a whole 2x2x4 slice. The times are simulated.
32 devices in a mesh: dp: 4 (over y, x), expert: 4 (over z), tensor: 2 (over core).
Axes of the slice: x: 2, y: 2, z: 4, core: 2. Of those that a mesh axis runs over, the one named last changes fastest.
Arguments:
- grad_out: bfloat16 [768, 7168], P(('dp', 'expert')), may hold values from -6 to 6
- gate_prob: bfloat16 [768, 2], P(('dp', 'expert')), may hold values from 0.049804688 to 0.94921875
- expert_ids: int32 [768, 2], P(('dp', 'expert')), may hold values from 0 to 3, as said below
- slot_positions: int32 [768, 2], P(('dp', 'expert')), may hold values from 0 to 38, as said below
- expert_down: bfloat16 [4, 2496, 7168], P('expert', 'tensor'), may hold values from -0.03125 to 0.03125
- dense_down: bfloat16 [2496, 7168], P(('expert', 'tensor')), may hold values from -0.03125 to 0.03125
- expert_gate_pre: bfloat16 [4, 624, 2496], P('expert', 'dp', 'tensor'), may hold values from -6 to 6
- expert_up_pre: bfloat16 [4, 624, 2496], P('expert', 'dp', 'tensor'), may hold values from -6 to 6
- dense_gate_pre: bfloat16 [768, 2496], P('dp', ('expert', 'tensor')), may hold values from -6 to 6
- dense_up_pre: bfloat16 [768, 2496], P('dp', ('expert', 'tensor')), may hold values from -6 to 6
Outputs:
- expert_gate_grad: bfloat16 [4, 624, 2496], P('expert', 'dp', 'tensor')
- expert_up_grad: bfloat16 [4, 624, 2496], P('expert', 'dp', 'tensor')
- slot_prob_grad: float32 [4, 624], P('expert', 'dp')
- expert_down_grad: bfloat16 [4, 7168, 2496], P('expert', 'dp', 'tensor')
- dense_gate_grad: bfloat16 [768, 2496], P('dp', ('expert', 'tensor'))
- dense_up_grad: bfloat16 [768, 2496], P('dp', ('expert', 'tensor'))
- dense_down_grad: bfloat16 [7168, 2496], P('dp', ('expert', 'tensor'))
Inputs may be any that keep to these rules, and one draw needn't show every extreme that they name: `expert_ids`: the two experts of a token differ. In each block of 48 tokens of one index of dp and expert, no expert is named more than 39 times, and one expert is named exactly 39 times; it is the same expert in all 4 blocks of one dp index. `slot_positions`: the rank of an assignment among the assignments of its block of 48 tokens to the same expert, counting tokens in order and a token's first expert before its second.
All inputs are finite; a program needn't handle non-finite values.
Results may differ from a plain program's by a relative error of at most 0.024.
Values may be sent and summed in bfloat16 or wider, within the bound.
A program may use at most 128 MiB of HBM per device.

v0:
```python
import jax
import jax.numpy as jnp
from jax import lax
from jax.sharding import PartitionSpec as P


def silu_parts(gate_val):
    gate_sig = jax.nn.sigmoid(gate_val)
    activated = gate_val * gate_sig
    slope = gate_sig * (1.0 + gate_val * (1.0 - gate_sig))
    return (activated, slope)


def local(
    grad_out,
    gate_prob,
    expert_ids,
    slot_positions,
    expert_down,
    dense_down,
    expert_gate_pre,
    expert_up_pre,
    dense_gate_pre,
    dense_up_pre,
):
    n_expert = lax.axis_size("expert")
    n_replica = lax.axis_size("dp")
    width = grad_out.shape[1]
    capacity = expert_gate_pre.shape[1] // n_expert
    flat_ids = expert_ids.reshape(-1)
    flat_slots = slot_positions.reshape(-1)
    repeated = jnp.repeat(grad_out, 2, axis=0)
    send_rows = (
        jnp.zeros((n_expert, capacity, width), jnp.bfloat16).at[flat_ids, flat_slots].set(repeated)
    )
    send_prob = (
        jnp.zeros((n_expert, capacity), jnp.bfloat16)
        .at[flat_ids, flat_slots]
        .set(gate_prob.reshape(-1))
    )
    recv_rows, recv_prob = (
        lax.all_to_all(send_rows, "expert", split_axis=0, concat_axis=0, tiled=True),
        lax.all_to_all(send_prob, "expert", split_axis=0, concat_axis=0, tiled=True),
    )
    slot_rows = recv_rows.reshape(n_expert * capacity, width)
    slot_prob = recv_prob.reshape(-1).astype(jnp.float32)
    weight_local = expert_down[0]
    back_hidden = lax.dot_general(
        slot_rows, weight_local, (((1,), (1,)), ((), ())), preferred_element_type=jnp.float32
    )
    gate_val = expert_gate_pre[0].astype(jnp.float32)
    up_val = expert_up_pre[0].astype(jnp.float32)
    activated, slope = silu_parts(gate_val)
    hidden = activated * up_val
    partial_dots = jnp.sum(back_hidden * hidden, axis=1)
    slot_dots = lax.psum(partial_dots, "tensor")
    scaled = slot_prob[:, None] * back_hidden
    expert_gate_grad = (scaled * up_val * slope).astype(jnp.bfloat16)[None]
    expert_up_grad = (scaled * activated).astype(jnp.bfloat16)[None]
    weighted = (slot_prob[:, None] * hidden).astype(jnp.bfloat16)
    expert_summed = lax.psum_scatter(
        lax.dot_general(
            slot_rows, weighted, (((0,), (0,)), ((), ())), preferred_element_type=jnp.float32
        ).astype(jnp.bfloat16),
        "dp",
        scatter_dimension=0,
        tiled=True,
    ).astype(jnp.float32)
    expert_down_grad = (expert_summed / n_replica).astype(jnp.bfloat16)[None]
    shard_rows = lax.all_gather(grad_out, "expert", axis=0, tiled=True)
    back_dense = lax.dot_general(
        shard_rows, dense_down, (((1,), (1,)), ((), ())), preferred_element_type=jnp.float32
    )
    dense_gate = dense_gate_pre.astype(jnp.float32)
    dense_up = dense_up_pre.astype(jnp.float32)
    dense_act, dense_slope = silu_parts(dense_gate)
    gate_buffer = (back_dense * dense_up * dense_slope).astype(jnp.bfloat16)
    up_buffer = (back_dense * dense_act).astype(jnp.bfloat16)
    dense_hidden = (dense_act * dense_up).astype(jnp.bfloat16)
    weight_sum = lax.dot_general(
        shard_rows, dense_hidden, (((0,), (0,)), ((), ())), preferred_element_type=jnp.float32
    )
    dense_summed = lax.psum_scatter(
        weight_sum.astype(jnp.bfloat16), "dp", scatter_dimension=0, tiled=True
    ).astype(jnp.float32)
    dense_down_grad = (dense_summed / n_replica).astype(jnp.bfloat16)
    return (
        expert_gate_grad,
        expert_up_grad,
        slot_dots[None],
        expert_down_grad,
        gate_buffer,
        up_buffer,
        dense_down_grad,
    )


def solution(mesh):
    return jax.shard_map(
        local,
        mesh=mesh,
        in_specs=(
            P(("dp", "expert"), None),
            P(("dp", "expert"), None),
            P(("dp", "expert"), None),
            P(("dp", "expert"), None),
            P("expert", "tensor", None),
            P(("expert", "tensor"), None),
            P("expert", "dp", "tensor"),
            P("expert", "dp", "tensor"),
            P("dp", ("expert", "tensor")),
            P("dp", ("expert", "tensor")),
        ),
        out_specs=(
            P("expert", "dp", "tensor"),
            P("expert", "dp", "tensor"),
            P("expert", "dp"),
            P("expert", "dp", "tensor"),
            P("dp", ("expert", "tensor")),
            P("dp", ("expert", "tensor")),
            P("dp", ("expert", "tensor")),
        ),
        check_vma=False,
    )
```

profile of v0, /device:TPU:1, one launch (start us, length us, event | category | flops | bytes accessed | tf_op | source)
XLA Modules:
  0.0 360.2 jit_solution(12690041178043722364)
XLA Ops:
  7.2 0.0 all-gather.2.cloned.1.call-start
  7.2 0.7 all-gather.2.cloned.1.call-update
  7.9 0.0 reduce-scatter.5.cloned.1.call-start
  7.9 60.7 %all-gather.2.cloned.1.call-done = bf16[192,7168]{1,0:T(8,128)(2,1)} async-done(((bf16[48,7168]{1,0:T(8,128)(2,1)}), bf16[192,7168]{1,0:T(8,128)(2,1)}) %all-gather.2.cloned.1.call-update) | async-done | bytes 2752528 | tf_op jit(solution)/shard_map/all_gather | solution.py:70
  68.6 5.4 %fusion.2 = bf16[7168,312]{0,1:T(8,128)(2,1)} fusion(bf16[192,7168]{1,0:T(8,128)(2,1)} %all-gather.2.cloned.1.call-done, bf16[192,312]{1,0:T(8,128)(2,1)} %param.19, bf16[192,312]{1,0:T(8,128)(2,1)} %param.18), kind=kOutput, calls=%fused_computation.7 | convolution fusion | flops 861499392 | bytes 7464960 | tf_op jit(solution)/shard_map/dot_general | solution.py:80
  74.1 0.0 copy-start.5
  74.1 0.0 copy-start.6
  74.1 0.0 copy-start.7
  74.1 0.0 copy-start
  74.1 0.0 reduce-scatter.5.cloned.1.call-update
  74.1 0.6 copy-done.5
  74.7 0.1 copy.24
  74.8 0.1 reshape.108
  75.0 0.0 copy-done.6
  75.0 0.1 copy.25
  75.1 0.1 reshape.109
  75.2 0.0 copy-done.7
  75.2 0.1 copy.26
  75.3 0.1 reshape.118
  75.5 5.1 %scatter_fusion = bf16[4,39]{1,0:T(4,128)(2,1)S(1)} fusion(bf16[4,39]{1,0:T(4,128)(2,1)S(1)} %broadcast_in_dim.27, s32[96]{0:T(128)S(1)} %fusion.38, bf16[96]{0:T(256)(128)(2,1)S(1)} %reshape.118), kind=kCustom, calls=%fused_computation | custom fusion | bytes 1344 | tf_op jit(solution)/shard_map/scatter | solution.py:39
  80.5 0.6 copy.27
  81.1 3.2 all-to-all-start
  84.3 0.0 copy-done
  84.3 0.7 broadcast_in_dim.29
  85.1 1.4 reshape.124
  86.5 0.6 broadcast_in_dim.28
  87.1 28.3 %scatter_fusion.1 = bf16[4,39,7168]{2,0,1:T(4,128)(2,1)S(1)} fusion(bf16[4,39,7168]{2,0,1:T(4,128)(2,1)S(1)} %broadcast_in_dim.28, s32[96]{0:T(128)S(1)} %fusion.38, bf16[96,7168]{1,0:T(8,128)(2,1)} %reshape.124), kind=kCustom, calls=%fused_computation.1 | custom fusion | bytes 4129536 | tf_op jit(solution)/shard_map/scatter | solution.py:34
  115.3 2.0 copy.28
  117.4 0.0 all-to-all-done
  117.4 4.5 %all-to-all-start.1 = ((bf16[4,39,7168]{2,1,0:T(8,128)(2,1)}), bf16[4,39,7168]{2,1,0:T(8,128)(2,1)}, u32[]{:S(2)}, u32[]{:S(2)}) async-start(bf16[4,39,7168]{2,1,0:T(8,128)(2,1)} %copy.28), calls=%async_computation.1 | async-start | bytes 4587520 | tf_op jit(solution)/shard_map/all_to_all | solution.py:42
  121.9 0.0 copy-start.1
  121.9 0.0 copy-start.2
  121.9 0.2 reduce-scatter.3.cloned.1.call-start
  122.2 0.1 reshape.113
  122.3 51.6 %all-to-all-done.1 = bf16[4,39,7168]{2,1,0:T(8,128)(2,1)} async-done(((bf16[4,39,7168]{2,1,0:T(8,128)(2,1)}), bf16[4,39,7168]{2,1,0:T(8,128)(2,1)}, u32[]{:S(2)}, u32[]{:S(2)}) %all-to-all-start.1) | async-done | bytes 2236448 | tf_op jit(solution)/shard_map/all_to_all | solution.py:42
  173.9 2.4 reshape.112
  176.3 0.0 copy-done.1
  176.3 0.0 copy-done.2
  176.3 8.9 %convolution_convert_fusion = bf16[7168,1248]{0,1:T(8,128)(2,1)} fusion(bf16[156,7168]{1,0:T(8,128)(2,1)S(1)} %reshape.112, bf16[1,156,1248]{2,1,0:T(8,128)(2,1)S(1)} %copy-done.1, bf16[1,156,1248]{2,1,0:T(8,128)(2,1)S(1)} %copy-done.2, f32[156]{0:T(256)S(1)} %reshape.113), kind=kOutput, calls=%fused_computation.2 | convolution fusion | flops 2801744896 | bytes 20907120 | tf_op jit(solution)/shard_map/dot_general | solution.py:62
  185.2 0.0 reduce-scatter.3.cloned.1.call-update
  185.2 0.0 copy-start.3
  185.2 0.0 copy-start.4
  185.2 13.1 %fusion.12 = (f32[156]{0:T(256)S(1)}, bf16[1,156,1248]{2,1,0:T(8,128)(2,1)}, bf16[1,156,1248]{2,1,0:T(8,128)(2,1)}) fusion(bf16[1,156,1248]{2,1,0:T(8,128)(2,1)S(1)} %copy-done.1, bf16[1,156,1248]{2,1,0:T(8,128)(2,1)S(1)} %copy-done.2, f32[156]{0:T(256)S(1)} %reshape.113, bf16[156,7168]{1,0:T(8,128)(2,1)S(1)} %reshape.112, bf16[1,1248,7168]{2,1,0:T(8,128)(2,1)} %param.14), kind=kOutput, calls=%fused_computation.23 | convolution fusion | flops 2794743808 | bytes 21686496 | tf_op jit(solution)/shard_map/dot_general | solution.py:48
  198.3 4.5 %psum.7 = f32[1,156]{1,0:T(1,128)} all-reduce(f32[1,156]{1,0:T(1,128)S(1)} %bitcast.72), channel_id=1, replica_groups=mesh['dp'=4,'expert'=4,'tensor'=2] {'tensor'}, use_global_device_ids=true, to_apply=%region_3.0 | all-reduce | flops 156 | bytes 1248 | tf_op jit(solution)/shard_map/psum | solution.py:56
  202.8 0.0 copy-done.3
  202.8 0.0 copy-done.4
  202.8 6.1 %multiply_convert_fusion.3 = (bf16[192,312]{1,0:T(8,128)(2,1)}, bf16[192,312]{1,0:T(8,128)(2,1)}) fusion(bf16[192,312]{1,0:T(8,128)(2,1)S(1)} %copy-done.4, bf16[192,312]{1,0:T(8,128)(2,1)S(1)} %copy-done.3, bf16[192,7168]{1,0:T(8,128)(2,1)} %all-gather.2.cloned.1.call-done, bf16[312,7168]{1,0:T(8,128)(2,1)} %param.15), kind=kOutput, calls=%fused_computation.52 | convolution fusion | flops 859682304 | bytes 7704576 | tf_op jit(solution)/shard_map/dot_general | solution.py:71
  208.9 0.0 reduce-scatter.5.cloned.1.call-done
  208.9 2.4 multiply_convert_fusion.1
  211.3 137.2 %reduce-scatter.3.cloned.1.call-done = bf16[1792,1248]{0,1:T(8,128)(2,1)} async-done(((bf16[7168,1248]{0,1:T(8,128)(2,1)}), bf16[1792,1248]{0,1:T(8,128)(2,1)}) %reduce-scatter.3.cloned.1.call-update) | async-done | bytes 4472848 | tf_op jit(solution)/shard_map/reduce_scatter | solution.py:61
  348.5 5.2 %fusion.3 = bf16[1,1792,1248]{1,2,0:T(8,128)(2,1)} fusion(bf16[1792,1248]{0,1:T(8,128)(2,1)} %reduce-scatter.3.cloned.1.call-done), kind=kLoop, calls=%fused_computation.8 | loop fusion | flops 6709248 | bytes 8945664 | tf_op jit(solution)/shard_map/broadcast_in_dim | solution.py:69
  (3 shorter events, 0.0 us)
Async XLA Ops:
  7.2 61.5 %all-gather.2.cloned.1.call-start = ((), (), s32[]{:S(2)}) async-start(), calls=%async_computation.5 | async-start | bytes 3440640 | tf_op jit(solution)/shard_map/all_gather | solution.py:70
  7.9 201.0 %reduce-scatter.5.cloned.1.call-start = ((), (), s32[]{:S(2)}) async-start(), calls=%async_computation.6 | async-start | bytes 5591040 | tf_op jit(solution)/shard_map/reduce_scatter | solution.py:83
  74.1 0.7 copy-start.5
  74.1 0.9 copy-start.6
  74.1 1.1 copy-start.7
  74.1 10.3 %copy-start = (bf16[48,7168]{1,0:T(8,128)(2,1)S(1)}, bf16[48,7168]{1,0:T(8,128)(2,1)}, u32[]{:S(2)}) copy-start(bf16[48,7168]{1,0:T(8,128)(2,1)} %param.10) | copy-start | bytes 2064388
  81.1 36.3 %all-to-all-start = ((bf16[4,1,39]{2,1,0:T(2,128)(2,1)}), bf16[4,1,39]{2,1,0:T(2,128)(2,1)S(1)}, u32[]{:S(2)}, u32[]{:S(2)}) async-start(bf16[4,1,39]{2,1,0:T(2,128)(2,1)} %copy.27), calls=%async_computation | async-start | bytes 4096 | tf_op jit(solution)/shard_map/all_to_all | solution.py:43
  117.4 56.5 %all-to-all-start.1 = ((bf16[4,39,7168]{2,1,0:T(8,128)(2,1)}), bf16[4,39,7168]{2,1,0:T(8,128)(2,1)}, u32[]{:S(2)}, u32[]{:S(2)}) async-start(bf16[4,39,7168]{2,1,0:T(8,128)(2,1)} %copy.28), calls=%async_computation.1 | async-start | bytes 4587520 | tf_op jit(solution)/shard_map/all_to_all | solution.py:42
  121.9 54.4 %copy-start.1 = (bf16[1,156,1248]{2,1,0:T(8,128)(2,1)S(1)}, bf16[1,156,1248]{2,1,0:T(8,128)(2,1)}, u32[]{:S(2)}) copy-start(bf16[1,156,1248]{2,1,0:T(8,128)(2,1)} %param.17) | copy-start | bytes 1168132
  121.9 54.4 %copy-start.2 = (bf16[1,156,1248]{2,1,0:T(8,128)(2,1)S(1)}, bf16[1,156,1248]{2,1,0:T(8,128)(2,1)}, u32[]{:S(2)}) copy-start(bf16[1,156,1248]{2,1,0:T(8,128)(2,1)} %param.16) | copy-start | bytes 1168132
  121.9 226.5 %reduce-scatter.3.cloned.1.call-start = ((), (), s32[]{:S(2)}) async-start(), calls=%async_computation.4 | async-start | bytes 22364160 | tf_op jit(solution)/shard_map/reduce_scatter | solution.py:61
  185.2 17.7 %copy-start.3 = (bf16[192,312]{1,0:T(8,128)(2,1)S(1)}, bf16[192,312]{1,0:T(8,128)(2,1)}, u32[]{:S(2)}) copy-start(bf16[192,312]{1,0:T(8,128)(2,1)} %param.19) | copy-start | bytes 359428
  185.2 17.6 %copy-start.4 = (bf16[192,312]{1,0:T(8,128)(2,1)S(1)}, bf16[192,312]{1,0:T(8,128)(2,1)}, u32[]{:S(2)}) copy-start(bf16[192,312]{1,0:T(8,128)(2,1)} %param.18) | copy-start | bytes 359428
Sparse Core Ops, SparseCore 0:
  9.6 59.0 all-gather.1
  74.2 54.2 reduce-scatter.4
  185.3 163.1 reduce-scatter.2
where the time goes:
time: 361 us; the launch traced here: 360 us
  waiting for transfers between devices  250 us (69%)
  local copies, waits for them, and re-layouts  42.4 us (12%)
  matrix products  33.4 us (9%)
  between operations  13.9 us (4%)
  starting transfers between devices  8.03 us (2%)
  other arithmetic  7.64 us (2%)
  blocking collectives  4.53 us (1%)
    reduce_scatter x1, waiting for transfers between devices, local(): lax.psum_scatter(lax.dot_general(slot_rows, weighted, (((0,), (0,)), ((),...  137 us
    all_gather x1, waiting for transfers between devices, local(): shard_rows = lax.all_gather(grad_out, 'expert', axis=0, tiled=True)  60.7 us
    all_to_all x1, waiting for transfers between devices, local(): lax.all_to_all(send_rows, 'expert', split_axis=0, concat_axis=0, tiled=True)  51.6 us
    scatter x2, local copies, waits for them, and re-layouts, local(): jnp.zeros((n_expert, capacity, width), jnp.bfloat16)  30.3 us
    dot_general x1, matrix products, local(): lax.dot_general(slot_rows, weight_local, (((1,), (1,)), ((), ())), prefer...  13.1 us
    dot_general x1, matrix products, local(): lax.dot_general(slot_rows, weighted, (((0,), (0,)), ((), ())), preferred_...  8.85 us
  transfers between devices with their start and end apart: 5, of which 3 were waited for; matrix products, arithmetic and copies ran while one was open for 20% of the time, Pallas kernels for 0%

commit v1 on v0

--- a/solution.py
+++ b/solution.py
@@ -1,7 +1,15 @@
+import functools
+
 import jax
 import jax.numpy as jnp
 from jax import lax
+from jax.experimental import pallas as pl
+from jax.experimental.pallas import tpu as pltpu
 from jax.sharding import PartitionSpec as P
+
+MESH = pl.DeviceIdType.MESH
+BF = jnp.bfloat16
+F32 = jnp.float32
 
 
 def silu_parts(gate_val):
@@ -11,7 +19,236 @@
     return (activated, slope)
 
 
-def local(
+def gather_kernel(
+    n_dp, n_z, grad, meta_in, hid_in, dh_in,
+    rows, slices, hid, dh, meta,
+    loc, z_send, z_recv, sib_send, sl_send, sl_recv, slf_send,
+    mz_send, mz_recv, md_send, md_recv, hid_send, hid_recv, dh_send, dh_recv,
+):
+    d, z, c = lax.axis_index("dp"), lax.axis_index("expert"), lax.axis_index("tensor")
+    half = n_dp // 2
+    unit = grad.shape[1] // n_dp
+    sib = (d, z, 1 - c)
+
+    def remote(src, dst, ssem, rsem, dev):
+        return pltpu.make_async_remote_copy(
+            src_ref=src, dst_ref=dst, send_sem=ssem, recv_sem=rsem, device_id=dev, device_id_type=MESH
+        )
+
+    def when(cond, fn):
+        if cond is True:
+            fn()
+        else:
+            pl.when(cond)(fn)
+
+    pending = []
+
+    def launch(cond, make):
+        when(cond, lambda: make().start())
+        pending.append((cond, make))
+
+    barrier = pltpu.get_barrier_semaphore()
+
+    def greet(dev):
+        pl.semaphore_signal(barrier, inc=1, device_id=dev, device_id_type=MESH)
+
+    peers = [lax.rem(d + k, n_dp) for k in range(1, n_dp)]
+    greet(sib)
+    for q in peers:
+        greet((q, z, c))
+    pl.when(z > 0)(lambda: greet((d, z - 1, c)))
+    pl.when(z < n_z - 1)(lambda: greet((d, z + 1, c)))
+    pl.semaphore_wait(barrier, n_dp + jnp.where(z > 0, 1, 0) + jnp.where(z < n_z - 1, 1, 0))
+
+    def cols(j):
+        return pl.ds(pl.multiple_of(j * unit, unit), unit)
+
+    def local_copies():
+        out = [
+            pltpu.make_async_copy(grad.at[:, pl.ds(j * unit, unit)], rows.at[j, z], loc.at[j])
+            for j in range(n_dp)
+        ]
+        out.append(pltpu.make_async_copy(hid_in, hid.at[d], loc.at[n_dp]))
+        out.append(pltpu.make_async_copy(dh_in, dh.at[d], loc.at[n_dp + 1]))
+        out.append(pltpu.make_async_copy(meta_in, meta.at[d, z], loc.at[n_dp + 2]))
+        return out
+
+    def spread(zb, jj, src, ok):
+        j = c * half + jj
+        launch(ok & (zb <= z) & (z < n_z - 1), lambda: remote(
+            src, rows.at[j, zb], z_send.at[0, jj, zb], z_recv.at[j, zb], (d, z + 1, c)))
+        launch(ok & (zb >= z) & (z > 0), lambda: remote(
+            src, rows.at[j, zb], z_send.at[1, jj, zb], z_recv.at[j, zb], (d, z - 1, c)))
+        launch(ok & (j != d), lambda: remote(
+            src, slices.at[d, zb], sl_send.at[jj, zb], sl_recv.at[d, zb], (j, z, c)))
+
+    def spread_meta(zb, src, ok):
+        launch(ok & (zb <= z) & (z < n_z - 1), lambda: remote(
+            src, meta.at[d, zb], mz_send.at[0, zb], mz_recv.at[zb], (d, z + 1, c)))
+        launch(ok & (zb >= z) & (z > 0), lambda: remote(
+            src, meta.at[d, zb], mz_send.at[1, zb], mz_recv.at[zb], (d, z - 1, c)))
+
+    yes = z >= 0
+    spread_meta(z, meta_in, yes)
+    for jj in range(half):
+        spread(z, jj, grad.at[:, cols(c * half + jj)], yes)
+    for k, q in enumerate(peers):
+        launch(True, lambda k=k, q=q: remote(
+            hid_in, hid.at[d], hid_send.at[k], hid_recv.at[d], (q, z, c)))
+        launch(True, lambda k=k, q=q: remote(
+            dh_in, dh.at[d], dh_send.at[k], dh_recv.at[d], (q, z, c)))
+    for copy in local_copies():
+        copy.start()
+
+    def arrived(dst, rsem):
+        return remote(dst, dst, loc.at[0], rsem, sib)
+
+    order = [(z + sign * dist, dist) for dist in range(1, n_z) for sign in (-1, 1)]
+    for zb, _ in order:
+        ok = (zb >= 0) & (zb < n_z)
+        pl.when(ok)(lambda: arrived(meta.at[d, zb], mz_recv.at[zb]).wait_recv())
+        spread_meta(zb, meta.at[d, zb], ok)
+        for jj in range(half):
+            j = c * half + jj
+            pl.when(ok)(lambda: arrived(rows.at[j, zb], z_recv.at[j, zb]).wait_recv())
+            spread(zb, jj, rows.at[j, zb], ok)
+            launch(ok, lambda zb=zb, jj=jj, j=j: remote(
+                rows.at[j, zb], rows.at[j, zb], sib_send.at[jj, zb], z_recv.at[j, zb], sib))
+    copies = local_copies()
+    for copy in copies:
+        copy.wait()
+    for k, q in enumerate(peers):
+        launch(True, lambda k=k, q=q: remote(
+            meta.at[d], meta.at[d], md_send.at[k], md_recv.at[d], (q, z, c)))
+    for zb, _ in order:
+        ok = (zb >= 0) & (zb < n_z)
+        for jj in range(half):
+            j = (1 - c) * half + jj
+            pl.when(ok)(lambda: arrived(rows.at[j, zb], z_recv.at[j, zb]).wait_recv())
+    own = pltpu.make_async_copy(rows.at[d], slices.at[d], loc.at[0])
+    own.start()
+    own_half = c == d // half
+    for zb, dist in [(z, 0)] + order:
+        ok = (zb >= 0) & (zb < n_z)
+        for q in peers:
+            pl.when(ok)(lambda: arrived(slices.at[q, zb], sl_recv.at[q, zb]).wait_recv())
+            launch(ok & own_half, lambda zb=zb, q=q: remote(
+                slices.at[q, zb], slices.at[q, zb], slf_send.at[q, zb], sl_recv.at[q, zb], sib))
+    for q in peers:
+        arrived(hid.at[q], hid_recv.at[q]).wait_recv()
+        arrived(dh.at[q], dh_recv.at[q]).wait_recv()
+        arrived(meta.at[q], md_recv.at[q]).wait_recv()
+    own.wait()
+    for cond, make in pending:
+        when(cond, lambda: make().wait_send())
+
+
+def gather_all(grad_out, meta_in, hid_in, dh_in, n_dp, n_z):
+    tok, width = grad_out.shape
+    unit = width // n_dp
+    half = n_dp // 2
+    vm = pl.BlockSpec(memory_space=pltpu.VMEM)
+    hbm = pl.BlockSpec(memory_space=pl.ANY)
+    dma = pltpu.SemaphoreType.DMA
+    return pl.pallas_call(
+        functools.partial(gather_kernel, n_dp, n_z),
+        out_shape=(
+            jax.ShapeDtypeStruct((n_dp, n_z, tok, unit), BF),
+            jax.ShapeDtypeStruct((n_dp, n_z, tok, unit), BF),
+            jax.ShapeDtypeStruct((n_dp,) + hid_in.shape, BF),
+            jax.ShapeDtypeStruct((n_dp,) + dh_in.shape, BF),
+            jax.ShapeDtypeStruct((n_dp, n_z) + meta_in.shape, BF),
+        ),
+        in_specs=[hbm, vm, vm, vm],
+        out_specs=(vm,) * 5,
+        scratch_shapes=[
+            dma((n_dp + 3,)),
+            dma((2, half, n_z)), dma((n_dp, n_z)), dma((half, n_z)),
+            dma((half, n_z)), dma((n_dp, n_z)), dma((n_dp, n_z)),
+            dma((2, n_z)), dma((n_z,)), dma((n_dp,)), dma((n_dp,)),
+            dma((n_dp,)), dma((n_dp,)), dma((n_dp,)), dma((n_dp,)),
+        ],
+        compiler_params=pltpu.CompilerParams(
+            collective_id=0, has_side_effects=True, vmem_limit_bytes=48 * 2**20
+        ),
+    )(grad_out, meta_in, hid_in, dh_in)
+
+
+def local_fast(
+    grad_out, gate_prob, expert_ids, slot_positions, expert_down, dense_down,
+    expert_gate_pre, expert_up_pre, dense_gate_pre, dense_up_pre,
+):
+    n_z = lax.axis_size("expert")
+    n_dp = lax.axis_size("dp")
+    me = lax.axis_index("expert")
+    tok, width = grad_out.shape
+    unit = width // n_dp
+    slots = expert_gate_pre.shape[1]
+    capacity = slots // n_z
+    padded = -(-slots // 16) * 16
+    meta_in = jnp.concatenate(
+        [expert_ids.astype(BF), slot_positions.astype(BF), gate_prob, jnp.zeros((tok, 122), BF)], axis=1
+    )
+    gate_val = expert_gate_pre[0].astype(F32)
+    up_val = expert_up_pre[0].astype(F32)
+    activated, slope = silu_parts(gate_val)
+    hidden = activated * up_val
+    dense_gate = dense_gate_pre.astype(F32)
+    dense_up = dense_up_pre.astype(F32)
+    dense_act, dense_slope = silu_parts(dense_gate)
+    hid_in = jnp.pad(hidden.astype(BF), ((0, padded - slots), (0, 0)))
+    dh_in = (dense_act * dense_up).astype(BF)
+
+    rows, slices, hid, dh, meta = gather_all(grad_out, meta_in, hid_in, dh_in, n_dp, n_z)
+
+    info = meta.reshape(n_dp, n_z * tok, 128).astype(F32)
+    block = (jnp.arange(n_z * tok) // tok * capacity).astype(F32)[None, :, None]
+    span = jnp.arange(padded).astype(F32)[None, None, :]
+    mine = me.astype(F32)
+    first = (info[:, :, 0:1] == mine) & (info[:, :, 2:3] + block == span)
+    second = (info[:, :, 1:2] == mine) & (info[:, :, 3:4] + block == span)
+    weight = jnp.where(first, info[:, :, 4:5], 0.0) + jnp.where(second, info[:, :, 5:6], 0.0)
+    here = lax.axis_index("dp")
+    pick = (first | second).astype(BF)
+    pick_d = lax.dynamic_index_in_dim(pick, here, 0, keepdims=False)
+    slot_prob = jnp.sum(lax.dynamic_index_in_dim(weight, here, 0, keepdims=False), axis=0)[:slots]
+
+    rows_tok = rows.reshape(n_dp, n_z * tok, unit)
+    routed = jnp.einsum("ts,jtu->sju", pick_d[:, :slots], rows_tok, preferred_element_type=BF)
+    back_hidden = lax.dot_general(
+        routed.reshape(slots, width), expert_down[0], (((1,), (1,)), ((), ())), preferred_element_type=F32
+    )
+    slot_dots = lax.psum(jnp.sum(back_hidden * hidden, axis=1), "tensor")
+    scaled = slot_prob[:, None] * back_hidden
+    expert_gate_grad = (scaled * up_val * slope).astype(BF)[None]
+    expert_up_grad = (scaled * activated).astype(BF)[None]
+    back_dense = jnp.einsum(
+        "jtu,hju->th", rows_tok, dense_down.reshape(-1, n_dp, unit), preferred_element_type=F32
+    )
+    dense_gate_grad = (back_dense * dense_up * dense_slope).astype(BF)
+    dense_up_grad = (back_dense * dense_act).astype(BF)
+
+    weighted = jnp.einsum("qts,qsh->qth", weight.astype(BF), hid, preferred_element_type=F32).astype(BF)
+    every = slices.reshape(-1, unit)
+    contract = (((0,), (0,)), ((), ()))
+    expert_sum = lax.dot_general(
+        every, weighted.reshape(every.shape[0], -1), contract, preferred_element_type=F32
+    )
+    dense_sum = lax.dot_general(
+        every, dh.reshape(every.shape[0], -1), contract, preferred_element_type=F32
+    )
+    return (
+        expert_gate_grad,
+        expert_up_grad,
+        slot_dots[None],
+        (expert_sum / n_dp).astype(BF)[None],
+        dense_gate_grad,
+        dense_up_grad,
+        (dense_sum / n_dp).astype(BF),
+    )
+
+
+def local_plain(
     grad_out,
     gate_prob,
     expert_ids,
@@ -96,6 +333,13 @@
 
 
 def solution(mesh):
+    sizes = mesh.shape
+    fits = sizes["tensor"] == 2 and sizes["dp"] == 4
+
+    def local(*args):
+        aligned = args[0].shape[1] % (sizes["dp"] * 128) == 0 and args[0].shape[0] % 16 == 0
+        return (local_fast if fits and aligned else local_plain)(*args)
+
     return jax.shard_map(
         local,
         mesh=mesh,

time: 361 us -> 97.5 us (0.27)
  waiting for transfers between devices: 250 us -> 0 us
  Pallas kernels: 0 us -> 50.4 us
  local copies, waits for them, and re-layouts: 42.4 us -> 13.3 us
  between operations: 13.9 us -> 0.79 us
  matrix products: 33.4 us -> 23.7 us
  starting transfers between devices: 8.03 us -> 0 us
    reduce_scatter x2 -> x0, waiting for transfers between devices: 137 us -> none  [the longest x1 137 us: local(): lax.psum_scatter(lax.dot_general(slot_rows, weighted, (((0,), (0,)), ((),...]
    all_gather x1 -> x0, waiting for transfers between devices: 60.7 us -> none  [local(): shard_rows = lax.all_gather(grad_out, 'expert', axis=0, tiled=True)]
    all_to_all x2 -> x0, waiting for transfers between devices: 51.7 us -> none  [the longest x1 51.6 us: local(): lax.all_to_all(send_rows, 'expert', split_axis=0, concat_axis=0, tiled=True)]
    pallas_call x0 -> x1, Pallas kernels: none -> 50.4 us  [gather_all(): pl.pallas_call(functools.partial(gather_kernel, n_dp, n_z), out_shape=(ja...]
    scatter x3 -> x0, local copies, waits for them, and re-layouts: 35.4 us -> none  [the longest x2 30.3 us: local(): jnp.zeros((n_expert, capacity, width), jnp.bfloat16)]
    dot_general x4 -> x5, matrix products: 33.4 us -> 23.7 us  [the longest x1 12.5 us: local_fast(): lax.dot_general(routed.reshape(slots, width), expert_down[0], (((1,), (1,...]
    all_to_all x2 -> x0, starting transfers between devices: 7.73 us -> none  [the longest x1 4.51 us: local(): lax.all_to_all(send_rows, 'expert', split_axis=0, concat_axis=0, tiled=True)]
    unnamed x19 -> x26, local copies, waits for them, and re-layouts: 0.97 us -> 7.74 us
  transfers between devices with their start and end apart: 5 -> 0, of which waited for: 3 -> 0; matrix products, arithmetic and copies ran while one was open for 20% -> 0% of each run, Pallas kernels for 0% -> 0%
where the time goes in v1:
time: 97.5 us; the launch traced here: 97.1 us
  Pallas kernels  50.4 us (52%)
  matrix products  23.7 us (24%)
  local copies, waits for them, and re-layouts  13.3 us (14%)
  other arithmetic  5.65 us (6%)
  blocking collectives  3.19 us (3%)
    pallas_call x1, Pallas kernels, gather_all(): pl.pallas_call(functools.partial(gather_kernel, n_dp, n_z), out_shape=(ja...  50.4 us
    dot_general x1, matrix products, local_fast(): lax.dot_general(routed.reshape(slots, width), expert_down[0], (((1,), (1,...  12.5 us
    unnamed x26, local copies, waits for them, and re-layouts  7.74 us
    dot_general x1, matrix products, local_fast(): lax.dot_general(every, weighted.reshape(every.shape[0], -1), contract, pr...  5.63 us
    reshape x1, local copies, waits for them, and re-layouts, local_fast(): rows_tok = rows.reshape(n_dp, n_z * tok, unit)  3.9 us
    psum x1, blocking collectives, local_fast(): slot_dots = lax.psum(jnp.sum(back_hidden * hidden, axis=1), 'tensor')  3.19 us
    dot_general x1, matrix products, local_fast(): jnp.einsum('jtu,hju->th', rows_tok, dense_down.reshape(-1, n_dp, unit), p...  2.72 us
    dot_general x1, matrix products, local_fast(): lax.dot_general(every, dh.reshape(every.shape[0], -1), contract, preferre...  2.14 us

profile of v1, /device:TPU:1, one launch (start us, length us, event | category | flops | bytes accessed | tf_op | source)
XLA Modules:
  0.0 97.1 jit_solution(12712916698518583300)
XLA Ops:
  0.6 0.0 copy-start
  0.6 1.5 %fusion.20 = bf16[156,1248]{1,0:T(8,128)(2,1)S(1)} fusion(bf16[1,156,1248]{2,1,0:T(8,128)(2,1)} %param.17, bf16[1,156,1248]{2,1,0:T(8,128)(2,1)} %param.16), kind=kLoop, calls=%fused_computation.30 | loop fusion | flops 1557504 | bytes 1168128 | tf_op jit(solution)/shard_map/convert_element_type | solution.py:199
  2.1 1.1 %fusion.24.dh_in = bf16[192,312]{1,0:T(8,128)(2,1)S(1)} fusion(bf16[192,312]{1,0:T(8,128)(2,1)} %param.19, bf16[192,312]{1,0:T(8,128)(2,1)} %param.18), kind=kLoop, calls=%fused_computation.41 | loop fusion | flops 479232 | bytes 359424 | tf_op jit(solution)/shard_map/convert_element_type | solution.py:200
  3.2 0.7 convert_element_type.84
  3.9 0.1 copy.21
  4.0 0.7 convert_element_type.85
  4.7 0.1 copy.22
  4.8 0.8 copy.23
  5.6 0.1 pad.8.clone
  5.7 0.1 maximum_maximum_fusion.meta_in
  5.7 0.0 copy-done
  5.7 50.4 %shard_map.153 = (bf16[4,4,48,1792]{3,2,1,0:T(8,128)(2,1)}, bf16[4,4,48,1792]{3,2,1,0:T(8,128)(2,1)}, bf16[4,160,1248]{2,1,0:T(8,128)(2,1)S(1)}, bf16[4,192,312]...) custom-call(bf16[48,7168]{1,0:T(8,128)(2,1)S(1)} %copy-done, bf16[48,128]{1,0:T(8,128)(2,1)S(1)} %maximum_maximum_fusion.meta_in, ...), custom_call_target="tpu_custom_call" | custom-call | tf_op jit(solution)/shard_map/pallas_call | solution.py:153
  56.2 1.3 %fusion.38 = (f32[4,192,1]{2,1,0:T(8,128)S(1)}, f32[4,192,1]{2,1,0:T(8,128)}, f32[4,192,1]{2,1,0:T(8,128)}, f32[4,192,1]{2,1,0:T(8,128)S(1)}) fusion(f32[4,192,128]{2,1,0:T(8,128)S(1)} %bitcast_convert_fusion), kind=kLoop, calls=%fused_computation.66 | loop fusion | bytes 24576 | tf_op jit(solution)/shard_map/slice | solution.py:210
  57.5 1.2 %copy.33 = f32[4,192,1]{1,0,2:T(4,128)S(1)} copy(f32[4,192,1]{2,1,0:T(8,128)} %get-tuple-element.24) | data formatting | bytes 6144
  58.7 1.2 %copy.36 = f32[4,192,1]{1,0,2:T(4,128)S(1)} copy(f32[4,192,1]{2,1,0:T(8,128)} %get-tuple-element.23) | data formatting | bytes 6144
  59.9 0.8 slice_compare_fusion.1
  60.8 1.1 %copy.40 = pred[4,192,1]{1,0,2:T(4,128)(4,1)S(1)} copy(pred[4,192,1]{2,1,0:T(8,128)(4,1)} %get-tuple-element.26) | data formatting | bytes 1536
  61.8 0.2 copy.41
  62.1 0.3 compare_and_fusion.1
  62.4 0.2 copy.37
  62.6 0.2 copy.34
  62.8 0.3 select_add_fusion
  63.1 0.1 dynamic-slice_reduce_fusion
  63.2 3.9 %copy.30 = bf16[4,192,1792]{2,0,1:T(4,128)(2,1)S(1)} copy(bf16[4,192,1792]{2,1,0:T(8,128)(2,1)} %bitcast.73) | data formatting | bytes 5505024 | tf_op jit(solution)/shard_map/reshape | solution.py:216
  67.1 0.0 copy-start.2
  67.2 0.0 copy-start.3
  67.2 1.9 %copy.39 = bf16[24,8,4,1792]{3,1,2,0:T(8,128)(2,1)} copy(bf16[24,8,4,1792]{3,2,1,0:T(4,128)(2,1)S(1)} %bitcast.72) | data formatting | bytes 5505024
  69.1 0.0 copy-done.2
  69.1 0.0 copy-done.3
  69.1 12.5 %multiply_reduce_fusion = (f32[156]{0:T(256)S(1)}, bf16[1,156,1248]{2,1,0:T(8,128)(2,1)}, bf16[1,156,1248]{2,1,0:T(8,128)(2,1)}) fusion(bf16[1,156,1248]{2,1,0:T(8,128)(2,1)S(1)} %copy-done.2, bf16[1,156,1248]{2,1,0:T(8,128)(2,1)S(1)} %copy-done.3, f32[156]{0:T(256)S(1)} %bitcast.86, bf16[1,1248,7168]{2,1,0:T(8,128)(2,1)} %param.14, ...), kind=kOutput, calls=%fused_computation.25 | convolution fusion | flops 3224135680 | bytes 22233312 | tf_op jit(solution)/shard_map/dot_general | solution.py:218
  81.6 3.2 %psum.7 = f32[1,156]{1,0:T(1,128)} all-reduce(f32[1,156]{1,0:T(1,128)S(1)} %bitcast.87), channel_id=1, replica_groups=mesh['dp'=4,'expert'=4,'tensor'=2] {'tensor'}, use_global_device_ids=true, to_apply=%region_2.3 | all-reduce | flops 156 | bytes 1248 | tf_op jit(solution)/shard_map/psum | solution.py:221
  84.8 0.0 copy-start.6
  84.8 0.0 slice-start
  84.8 0.8 convolution_convert_fusion
  85.6 1.0 copy-done.6
  86.5 0.0 slice-start.1
  86.5 5.6 %fusion.3 = bf16[1,1792,1248]{1,2,0:T(8,128)(2,1)} fusion(bf16[768,1792]{1,0:T(8,128)(2,1)S(1)} %bitcast.91, bf16[768,1248]{1,0:T(8,128)(2,1)S(1)} %bitcast.93), kind=kOutput, calls=%fused_computation.4 | convolution fusion | flops 3439607808 | bytes 9142272 | tf_op jit(solution)/shard_map/dot_general | solution.py:234
  92.2 0.0 copy-start.1
  92.2 0.0 copy-start.4
  92.2 0.0 copy-start.5
  92.2 2.1 %fusion.7 = bf16[1792,312]{0,1:T(8,128)(2,1)} fusion(bf16[768,1792]{1,0:T(8,128)(2,1)S(1)} %bitcast.92, bf16[768,312]{1,0:T(8,128)(2,1)S(1)} %bitcast.71), kind=kOutput, calls=%fused_computation.10 | convolution fusion | flops 859901952 | bytes 4349952 | tf_op jit(solution)/shard_map/dot_general | solution.py:237
  94.3 0.0 slice-done
  94.3 0.0 slice-done.1
  94.3 0.0 copy-done.1
  94.3 0.0 copy-done.4
  94.3 0.0 copy-done.5
  94.3 2.7 %multiply_convert_fusion.1 = (bf16[192,312]{1,0:T(8,128)(2,1)}, bf16[192,312]{1,0:T(8,128)(2,1)}) fusion(bf16[192,312]{1,0:T(8,128)(2,1)S(1)} %copy-done.5, bf16[192,312]{1,0:T(8,128)(2,1)S(1)} %copy-done.4, bf16[4,192,1792]{2,1,0:T(8,128)(2,1)S(1)} %bitcast.74, bf16[39,4,8,1792]{3,2,1,0:T(8,128)(2,1)S(1)} %bitcast.90), kind=kOutput, calls=%fused_computation.49 | convolution fusion | flops 859682304 | bytes 7704576 | tf_op jit(solution)/shard_map/jtu,hju->th/dot_general | solution.py:225
  (8 shorter events, 0.1 us)
Async XLA Ops:
  0.6 5.1 %copy-start = (bf16[48,7168]{1,0:T(8,128)(2,1)S(1)}, bf16[48,7168]{1,0:T(8,128)(2,1)}, u32[]{:S(2)}) copy-start(bf16[48,7168]{1,0:T(8,128)(2,1)} %grad.1) | copy-start | bytes 2064388
  67.1 2.0 %copy-start.2 = (bf16[1,156,1248]{2,1,0:T(8,128)(2,1)S(1)}, bf16[1,156,1248]{2,1,0:T(8,128)(2,1)}, u32[]{:S(2)}) copy-start(bf16[1,156,1248]{2,1,0:T(8,128)(2,1)} %param.17) | copy-start | bytes 1168132
  67.2 2.0 %copy-start.3 = (bf16[1,156,1248]{2,1,0:T(8,128)(2,1)S(1)}, bf16[1,156,1248]{2,1,0:T(8,128)(2,1)}, u32[]{:S(2)}) copy-start(bf16[1,156,1248]{2,1,0:T(8,128)(2,1)} %param.16) | copy-start | bytes 1168132
  84.8 1.8 %copy-start.6 = (bf16[4,4,48,1792]{3,2,1,0:T(8,128)(2,1)S(1)}, bf16[4,4,48,1792]{3,2,1,0:T(8,128)(2,1)}, u32[]{:S(2)}) copy-start(bf16[4,4,48,1792]{3,2,1,0:T(8,128)(2,1)} %get-tuple-element.14) | copy-start | bytes 8257540
  84.8 9.6 %slice-start = ((s8[4472832]{0:T(1024)(128)(4,1)}), s8[4194304]{0:T(1024)(128)(4,1)S(1)}, s32[]{:S(2)}) async-start(s8[4472832]{0:T(1024)(128)(4,1)} %bitcast.88), calls=%async_computation | async-start | bytes 8388608
  86.5 7.8 %slice-start.1 = ((s8[4472832]{0:T(1024)(128)(4,1)}), s8[278528]{0:T(1024)(128)(4,1)S(1)}, s32[]{:S(2)}) async-start(s8[4472832]{0:T(1024)(128)(4,1)} %bitcast.88), calls=%async_computation.1 | async-start | bytes 557056
  92.2 2.2 %copy-start.1 = (bf16[4,4,48,1792]{3,2,1,0:T(8,128)(2,1)S(1)}, bf16[4,4,48,1792]{3,2,1,0:T(8,128)(2,1)}, u32[]{:S(2)}) copy-start(bf16[4,4,48,1792]{3,2,1,0:T(8,128)(2,1)} %get-tuple-element.13) | copy-start | bytes 8257540
  92.2 2.2 %copy-start.4 = (bf16[192,312]{1,0:T(8,128)(2,1)S(1)}, bf16[192,312]{1,0:T(8,128)(2,1)}, u32[]{:S(2)}) copy-start(bf16[192,312]{1,0:T(8,128)(2,1)} %param.19) | copy-start | bytes 359428
  92.2 2.2 %copy-start.5 = (bf16[192,312]{1,0:T(8,128)(2,1)S(1)}, bf16[192,312]{1,0:T(8,128)(2,1)}, u32[]{:S(2)}) copy-start(bf16[192,312]{1,0:T(8,128)(2,1)} %param.18) | copy-start | bytes 359428

commit v2 on v1

--- a/solution.py
+++ b/solution.py
@@ -19,16 +19,38 @@
     return (activated, slope)
 
 
-def gather_kernel(
-    n_dp, n_z, grad, meta_in, hid_in, dh_in,
-    rows, slices, hid, dh, meta,
-    loc, z_send, z_recv, sib_send, sl_send, sl_recv, slf_send,
+def selection(info, mine, capacity, slots, tok):
+    info = info.astype(F32)
+    tokens = info.shape[0]
+    block = lax.broadcasted_iota(jnp.int32, (tokens, slots), 0) // tok
+    span = (lax.broadcasted_iota(jnp.int32, (tokens, slots), 1) - block * capacity).astype(F32)
+    first = (info[:, 0:1] == mine) & (info[:, 2:3] == span)
+    second = (info[:, 1:2] == mine) & (info[:, 3:4] == span)
+    weight = jnp.where(first, info[:, 4:5], 0.0) + jnp.where(second, info[:, 5:6], 0.0)
+    pick = jnp.where(first | second, 1.0, 0.0)
+    return pick.astype(BF), weight.astype(BF)
+
+
+def layer_kernel(
+    n_dp, n_z, grad, meta_in, expert_w, dense_w, gate_pre, up_pre, dense_gate_pre, dense_up_pre,
+    slices, weighted, dh, gate_out, up_out, dgate_out, dup_out, dots_out,
+    rows, hid, meta, w, dw, acc, dacc, dots,
+    loc, w_sem, dw_sem, z_send, z_recv, sib_send, sl_send, sl_recv, slf_send,
     mz_send, mz_recv, md_send, md_recv, hid_send, hid_recv, dh_send, dh_recv,
+    hf_send, hf_recv, df_send, df_recv, dot_send, dot_recv,
 ):
     d, z, c = lax.axis_index("dp"), lax.axis_index("expert"), lax.axis_index("tensor")
     half = n_dp // 2
+    tok = grad.shape[0]
     unit = grad.shape[1] // n_dp
+    slots = gate_pre.shape[1]
+    padded = hid.shape[1]
+    capacity = slots // n_z
     sib = (d, z, 1 - c)
+    flip_x = d + 1 - 2 * lax.rem(d, 2)
+    flip_y = lax.rem(d + 2, n_dp)
+    diag = lax.rem(flip_x + 2, n_dp)
+    peers = [flip_x, flip_y, diag]
 
     def remote(src, dst, ssem, rsem, dev):
         return pltpu.make_async_remote_copy(
@@ -52,13 +74,11 @@
     def greet(dev):
         pl.semaphore_signal(barrier, inc=1, device_id=dev, device_id_type=MESH)
 
-    peers = [lax.rem(d + k, n_dp) for k in range(1, n_dp)]
     greet(sib)
     for q in peers:
         greet((q, z, c))
     pl.when(z > 0)(lambda: greet((d, z - 1, c)))
     pl.when(z < n_z - 1)(lambda: greet((d, z + 1, c)))
-    pl.semaphore_wait(barrier, n_dp + jnp.where(z > 0, 1, 0) + jnp.where(z < n_z - 1, 1, 0))
 
     def cols(j):
         return pl.ds(pl.multiple_of(j * unit, unit), unit)
@@ -68,10 +88,25 @@
             pltpu.make_async_copy(grad.at[:, pl.ds(j * unit, unit)], rows.at[j, z], loc.at[j])
             for j in range(n_dp)
         ]
-        out.append(pltpu.make_async_copy(hid_in, hid.at[d], loc.at[n_dp]))
-        out.append(pltpu.make_async_copy(dh_in, dh.at[d], loc.at[n_dp + 1]))
-        out.append(pltpu.make_async_copy(meta_in, meta.at[d, z], loc.at[n_dp + 2]))
+        out.append(pltpu.make_async_copy(meta_in, meta.at[d, z], loc.at[n_dp]))
         return out
+
+    def weight_copies(j):
+        return (
+            pltpu.make_async_copy(expert_w.at[0, :, cols(j)], w.at[j], w_sem.at[j]),
+            pltpu.make_async_copy(dense_w.at[:, cols(j)], dw.at[j], dw_sem.at[j]),
+        )
+
+    for copy in local_copies():
+        copy.start()
+
+    hid[d] = jnp.zeros(hid.shape[1:], BF)
+    activated, _ = silu_parts(gate_pre[0].astype(F32))
+    hid[d, pl.ds(0, slots), :] = (activated * up_pre[0].astype(F32)).astype(BF)
+    activated, _ = silu_parts(dense_gate_pre[...].astype(F32))
+    dh[d] = (activated * dense_up_pre[...].astype(F32)).astype(BF)
+
+    pl.semaphore_wait(barrier, n_dp + jnp.where(z > 0, 1, 0) + jnp.where(z < n_z - 1, 1, 0))
 
     def spread(zb, jj, src, ok):
         j = c * half + jj
@@ -92,19 +127,41 @@
     spread_meta(z, meta_in, yes)
     for jj in range(half):
         spread(z, jj, grad.at[:, cols(c * half + jj)], yes)
-    for k, q in enumerate(peers):
+    for k, q in enumerate(peers[:2]):
         launch(True, lambda k=k, q=q: remote(
-            hid_in, hid.at[d], hid_send.at[k], hid_recv.at[d], (q, z, c)))
+            hid.at[d], hid.at[d], hid_send.at[k], hid_recv.at[d], (q, z, c)))
         launch(True, lambda k=k, q=q: remote(
-            dh_in, dh.at[d], dh_send.at[k], dh_recv.at[d], (q, z, c)))
-    for copy in local_copies():
-        copy.start()
+            dh.at[d], dh.at[d], dh_send.at[k], dh_recv.at[d], (q, z, c)))
+    for j in range(n_dp):
+        for copy in weight_copies(j):
+            copy.start()
 
     def arrived(dst, rsem):
         return remote(dst, dst, loc.at[0], rsem, sib)
 
+    def pass_hidden():
+        for k, (source, target) in enumerate(((flip_x, flip_y), (flip_y, flip_x))):
+            arrived(hid.at[source], hid_recv.at[source]).wait_recv()
+            arrived(dh.at[source], dh_recv.at[source]).wait_recv()
+            part = pl.ds(k * (padded // 2), padded // 2)
+            dpart = pl.ds(k * (dh.shape[1] // 2), dh.shape[1] // 2)
+            launch(True, lambda k=k, source=source, target=target, part=part: remote(
+                hid.at[source, part], hid.at[source, part], hf_send.at[k], hf_recv.at[k], (target, z, c)))
+            launch(True, lambda k=k, source=source, target=target, dpart=dpart: remote(
+                dh.at[source, dpart], dh.at[source, dpart], df_send.at[k], df_recv.at[k], (target, z, c)))
+
+    own_half = c == d // half
+
+    def pass_slices(zb, ok):
+        for q in peers:
+            pl.when(ok)(lambda: arrived(slices.at[q, zb], sl_recv.at[q, zb]).wait_recv())
+            launch(ok & own_half, lambda q=q: remote(
+                slices.at[q, zb], slices.at[q, zb], slf_send.at[q, zb], sl_recv.at[q, zb], sib))
+
     order = [(z + sign * dist, dist) for dist in range(1, n_z) for sign in (-1, 1)]
-    for zb, _ in order:
+    for step, (zb, dist) in enumerate(order):
+        if step == 2 * (n_z - 2):
+            pass_hidden()
         ok = (zb >= 0) & (zb < n_z)
         pl.when(ok)(lambda: arrived(meta.at[d, zb], mz_recv.at[zb]).wait_recv())
         spread_meta(zb, meta.at[d, zb], ok)
@@ -114,12 +171,14 @@
             spread(zb, jj, rows.at[j, zb], ok)
             launch(ok, lambda zb=zb, jj=jj, j=j: remote(
                 rows.at[j, zb], rows.at[j, zb], sib_send.at[jj, zb], z_recv.at[j, zb], sib))
-    copies = local_copies()
-    for copy in copies:
+    for copy in local_copies():
         copy.wait()
     for k, q in enumerate(peers):
         launch(True, lambda k=k, q=q: remote(
             meta.at[d], meta.at[d], md_send.at[k], md_recv.at[d], (q, z, c)))
+    pass_slices(z, yes)
+    for zb, dist in order[:2]:
+        pass_slices(zb, (zb >= 0) & (zb < n_z))
     for zb, _ in order:
         ok = (zb >= 0) & (zb < n_z)
         for jj in range(half):
@@ -127,51 +186,114 @@
             pl.when(ok)(lambda: arrived(rows.at[j, zb], z_recv.at[j, zb]).wait_recv())
     own = pltpu.make_async_copy(rows.at[d], slices.at[d], loc.at[0])
     own.start()
-    own_half = c == d // half
-    for zb, dist in [(z, 0)] + order:
-        ok = (zb >= 0) & (zb < n_z)
-        for q in peers:
-            pl.when(ok)(lambda: arrived(slices.at[q, zb], sl_recv.at[q, zb]).wait_recv())
-            launch(ok & own_half, lambda zb=zb, q=q: remote(
-                slices.at[q, zb], slices.at[q, zb], slf_send.at[q, zb], sl_recv.at[q, zb], sib))
+
+    mine = z.astype(F32)
+    info = meta[d].reshape(n_z * tok, meta.shape[-1])
+    pick, weight = selection(info, mine, capacity, padded, tok)
+    by_token = (((0,), (0,)), ((), ()))
+    by_width = (((1,), (1,)), ((), ()))
+    acc[...] = jnp.zeros_like(acc)
+    dacc[...] = jnp.zeros_like(dacc)
+
+    def back(j, _):
+        for copy in weight_copies(j):
+            copy.wait()
+        tokens = rows[j].reshape(n_z * tok, unit)
+        routed = lax.dot_general(pick, tokens, by_token, preferred_element_type=F32).astype(BF)
+        acc[...] += lax.dot_general(routed, w[j], by_width, preferred_element_type=F32)
+        dacc[...] += lax.dot_general(tokens, dw[j], by_width, preferred_element_type=F32)
+        return 0
+
+    lax.fori_loop(0, n_dp, back, 0)
+
+    prob = lax.dot_general(
+        weight, jnp.ones((n_z * tok, 128), BF), by_token, preferred_element_type=F32
+    )[:slots, 0:1]
+    back_hidden = acc[pl.ds(0, slots), :]
+    up_val = up_pre[0].astype(F32)
+    activated, slope = silu_parts(gate_pre[0].astype(F32))
+    partial = jnp.sum(back_hidden * (activated * up_val), axis=1, keepdims=True)
+    dots[0] = jnp.zeros(dots.shape[1:], F32)
+    dots[0, pl.ds(0, slots), :] = jnp.broadcast_to(partial, (slots, 128))
+    launch(True, lambda: remote(dots.at[0], dots.at[1], dot_send, dot_recv, sib))
+    for zb, dist in order[2:]:
+        pass_slices(zb, (zb >= 0) & (zb < n_z))
+    scaled = prob * back_hidden
+    gate_out[0] = (scaled * up_val * slope).astype(BF)
+    up_out[0] = (scaled * activated).astype(BF)
+    dense_up = dense_up_pre[...].astype(F32)
+    activated, slope = silu_parts(dense_gate_pre[...].astype(F32))
+    dgate_out[...] = (dacc[...] * dense_up * slope).astype(BF)
+    dup_out[...] = (dacc[...] * activated).astype(BF)
+
     for q in peers:
-        arrived(hid.at[q], hid_recv.at[q]).wait_recv()
-        arrived(dh.at[q], dh_recv.at[q]).wait_recv()
         arrived(meta.at[q], md_recv.at[q]).wait_recv()
+    for k in range(2):
+        part = pl.ds(k * (padded // 2), padded // 2)
+        dpart = pl.ds(k * (dh.shape[1] // 2), dh.shape[1] // 2)
+        arrived(hid.at[diag, part], hf_recv.at[k]).wait_recv()
+        arrived(dh.at[diag, dpart], df_recv.at[k]).wait_recv()
+
+    def place(q, _):
+        _, weight_q = selection(
+            meta[q].reshape(n_z * tok, meta.shape[-1]), mine, capacity, padded, tok
+        )
+        weighted[q] = jnp.dot(weight_q, hid[q], preferred_element_type=F32).astype(BF)
+        return 0
+
+    lax.fori_loop(0, n_dp, place, 0)
+    arrived(dots.at[1], dot_recv).wait_recv()
+    dots_out[...] = dots[0] + dots[1]
     own.wait()
     for cond, make in pending:
         when(cond, lambda: make().wait_send())
 
 
-def gather_all(grad_out, meta_in, hid_in, dh_in, n_dp, n_z):
+def layer(grad_out, meta_in, expert_down, dense_down, gate_pre, up_pre, dense_gate, dense_up, n_dp, n_z):
     tok, width = grad_out.shape
     unit = width // n_dp
     half = n_dp // 2
+    _, slots, he = gate_pre.shape
+    tokens, hd = dense_gate.shape
+    padded = -(-slots // 32) * 32
     vm = pl.BlockSpec(memory_space=pltpu.VMEM)
     hbm = pl.BlockSpec(memory_space=pl.ANY)
     dma = pltpu.SemaphoreType.DMA
+    shape = jax.ShapeDtypeStruct
     return pl.pallas_call(
-        functools.partial(gather_kernel, n_dp, n_z),
+        functools.partial(layer_kernel, n_dp, n_z),
         out_shape=(
-            jax.ShapeDtypeStruct((n_dp, n_z, tok, unit), BF),
-            jax.ShapeDtypeStruct((n_dp, n_z, tok, unit), BF),
-            jax.ShapeDtypeStruct((n_dp,) + hid_in.shape, BF),
-            jax.ShapeDtypeStruct((n_dp,) + dh_in.shape, BF),
-            jax.ShapeDtypeStruct((n_dp, n_z) + meta_in.shape, BF),
+            shape((n_dp, n_z, tok, unit), BF),
+            shape((n_dp, tokens, he), BF),
+            shape((n_dp, tokens, hd), BF),
+            shape(gate_pre.shape, BF),
+            shape(gate_pre.shape, BF),
+            shape(dense_gate.shape, BF),
+            shape(dense_gate.shape, BF),
+            shape((padded, 128), F32),
         ),
-        in_specs=[hbm, vm, vm, vm],
-        out_specs=(vm,) * 5,
+        in_specs=[hbm, vm, hbm, hbm, vm, vm, vm, vm],
+        out_specs=(vm,) * 8,
         scratch_shapes=[
-            dma((n_dp + 3,)),
+            pltpu.VMEM((n_dp, n_z, tok, unit), BF),
+            pltpu.VMEM((n_dp, padded, he), BF),
+            pltpu.VMEM((n_dp, n_z) + meta_in.shape, BF),
+            pltpu.VMEM((n_dp, he, unit), BF),
+            pltpu.VMEM((n_dp, hd, unit), BF),
+            pltpu.VMEM((padded, he), F32),
+            pltpu.VMEM((tokens, hd), F32),
+            pltpu.VMEM((2, padded, 128), F32),
+            dma((n_dp + 1,)), dma((n_dp,)), dma((n_dp,)),
             dma((2, half, n_z)), dma((n_dp, n_z)), dma((half, n_z)),
             dma((half, n_z)), dma((n_dp, n_z)), dma((n_dp, n_z)),
             dma((2, n_z)), dma((n_z,)), dma((n_dp,)), dma((n_dp,)),
-            dma((n_dp,)), dma((n_dp,)), dma((n_dp,)), dma((n_dp,)),
+            dma((2,)), dma((n_dp,)), dma((2,)), dma((n_dp,)),
+            dma((2,)), dma((2,)), dma((2,)), dma((2,)), dma, dma,
         ],
         compiler_params=pltpu.CompilerParams(
-            collective_id=0, has_side_effects=True, vmem_limit_bytes=48 * 2**20
+            collective_id=0, has_side_effects=True, vmem_limit_bytes=58 * 2**20
         ),
-    )(grad_out, meta_in, hid_in, dh_in)
+    )(grad_out, meta_in, expert_down, dense_down, gate_pre, up_pre, dense_gate, dense_up)
 
 
 def local_fast(
@@ -180,56 +302,16 @@
 ):
     n_z = lax.axis_size("expert")
     n_dp = lax.axis_size("dp")
-    me = lax.axis_index("expert")
-    tok, width = grad_out.shape
-    unit = width // n_dp
+    tok = grad_out.shape[0]
     slots = expert_gate_pre.shape[1]
-    capacity = slots // n_z
-    padded = -(-slots // 16) * 16
     meta_in = jnp.concatenate(
         [expert_ids.astype(BF), slot_positions.astype(BF), gate_prob, jnp.zeros((tok, 122), BF)], axis=1
     )
-    gate_val = expert_gate_pre[0].astype(F32)
-    up_val = expert_up_pre[0].astype(F32)
-    activated, slope = silu_parts(gate_val)
-    hidden = activated * up_val
-    dense_gate = dense_gate_pre.astype(F32)
-    dense_up = dense_up_pre.astype(F32)
-    dense_act, dense_slope = silu_parts(dense_gate)
-    hid_in = jnp.pad(hidden.astype(BF), ((0, padded - slots), (0, 0)))
-    dh_in = (dense_act * dense_up).astype(BF)
-
-    rows, slices, hid, dh, meta = gather_all(grad_out, meta_in, hid_in, dh_in, n_dp, n_z)
-
-    info = meta.reshape(n_dp, n_z * tok, 128).astype(F32)
-    block = (jnp.arange(n_z * tok) // tok * capacity).astype(F32)[None, :, None]
-    span = jnp.arange(padded).astype(F32)[None, None, :]
-    mine = me.astype(F32)
-    first = (info[:, :, 0:1] == mine) & (info[:, :, 2:3] + block == span)
-    second = (info[:, :, 1:2] == mine) & (info[:, :, 3:4] + block == span)
-    weight = jnp.where(first, info[:, :, 4:5], 0.0) + jnp.where(second, info[:, :, 5:6], 0.0)
-    here = lax.axis_index("dp")
-    pick = (first | second).astype(BF)
-    pick_d = lax.dynamic_index_in_dim(pick, here, 0, keepdims=False)
-    slot_prob = jnp.sum(lax.dynamic_index_in_dim(weight, here, 0, keepdims=False), axis=0)[:slots]
-
-    rows_tok = rows.reshape(n_dp, n_z * tok, unit)
-    routed = jnp.einsum("ts,jtu->sju", pick_d[:, :slots], rows_tok, preferred_element_type=BF)
-    back_hidden = lax.dot_general(
-        routed.reshape(slots, width), expert_down[0], (((1,), (1,)), ((), ())), preferred_element_type=F32
-    )
-    slot_dots = lax.psum(jnp.sum(back_hidden * hidden, axis=1), "tensor")
-    scaled = slot_prob[:, None] * back_hidden
-    expert_gate_grad = (scaled * up_val * slope).astype(BF)[None]
-    expert_up_grad = (scaled * activated).astype(BF)[None]
-    back_dense = jnp.einsum(
-        "jtu,hju->th", rows_tok, dense_down.reshape(-1, n_dp, unit), preferred_element_type=F32
-    )
-    dense_gate_grad = (back_dense * dense_up * dense_slope).astype(BF)
-    dense_up_grad = (back_dense * dense_act).astype(BF)
-
-    weighted = jnp.einsum("qts,qsh->qth", weight.astype(BF), hid, preferred_element_type=F32).astype(BF)
-    every = slices.reshape(-1, unit)
+    slices, weighted, dh, gate_grad, up_grad, dgate_grad, dup_grad, dots = layer(
+        grad_out, meta_in, expert_down, dense_down,
+        expert_gate_pre, expert_up_pre, dense_gate_pre, dense_up_pre, n_dp, n_z,
+    )
+    every = slices.reshape(-1, slices.shape[-1])
     contract = (((0,), (0,)), ((), ()))
     expert_sum = lax.dot_general(
         every, weighted.reshape(every.shape[0], -1), contract, preferred_element_type=F32
@@ -238,12 +320,12 @@
         every, dh.reshape(every.shape[0], -1), contract, preferred_element_type=F32
     )
     return (
-        expert_gate_grad,
-        expert_up_grad,
-        slot_dots[None],
+        gate_grad,
+        up_grad,
+        dots[:slots, 0][None],
         (expert_sum / n_dp).astype(BF)[None],
-        dense_gate_grad,
-        dense_up_grad,
+        dgate_grad,
+        dup_grad,
         (dense_sum / n_dp).astype(BF),
     )
 

time: 97.5 us -> 68.8 us (0.71)
  the two profiles are of different devices: /device:TPU:1 before, /device:TPU:11 now
where the time goes in v2:
time: 68.8 us; the launch traced here: 68.5 us
  Pallas kernels  49.9 us (73%)
  matrix products  10.4 us (15%)
  local copies, waits for them, and re-layouts  5.47 us (8%)
  other arithmetic  2.05 us (3%)
    pallas_call x1, Pallas kernels, layer(): pl.pallas_call(functools.partial(layer_kernel, n_dp, n_z), out_shape=(sha...  49.9 us
    dot_general x1, matrix products, local_fast(): lax.dot_general(every, weighted.reshape(every.shape[0], -1), contract, pr...  8.31 us
    unnamed x17, local copies, waits for them, and re-layouts  3.6 us
    dot_general x1, matrix products, local_fast(): lax.dot_general(every, dh.reshape(every.shape[0], -1), contract, preferre...  2.13 us
    slice x1, local copies, waits for them, and re-layouts, local_fast(): dots[:slots, 0][None]  1.56 us

profile of v2, /device:TPU:11, one launch (start us, length us, event | category | flops | bytes accessed | tf_op | source)
XLA Modules:
  0.0 68.5 jit_solution(4931137712044425397)
XLA Ops:
  0.6 0.8 %copy.22 = bf16[48,2]{1,0:T(8,128)(2,1)S(1)} copy(bf16[48,2]{0,1:T(2,128)(2,1)} %param.11) | data formatting | bytes 384 | tf_op args[1]
  1.4 0.7 convert_element_type.13
  2.1 0.1 copy.21
  2.2 0.7 convert_element_type.12
  2.9 0.1 copy.20
  3.0 0.1 pad.3.clone
  3.1 0.7 maximum_maximum_fusion.meta_in
  3.7 49.9 %shard_map.153 = (bf16[4,4,48,1792]{3,2,1,0:T(8,128)(2,1)}, bf16[4,192,1248]{2,1,0:T(8,128)(2,1)}, bf16[4,192,312]{2,1,0:T(8,128)(2,1)}, bf16[1,156,1248]{2,1,0:...) custom-call(bf16[48,7168]{1,0:T(8,128)(2,1)} %grad.1, ...), custom_call_target="tpu_custom_call" | custom-call | tf_op jit(solution)/shard_map/pallas_call | solution.py:263
  53.7 1.6 %slice_reduce_fusion = f32[156]{0:T(256)} fusion(f32[160,128]{1,0:T(8,128)} %get-tuple-element.17), kind=kLoop, calls=%fused_computation.5 | loop fusion | bytes 1248 | tf_op jit(solution)/shard_map/slice | solution.py:325
  55.2 0.0 copy-start.4
  55.2 0.0 copy-start.5
  55.2 8.3 %fusion.1 = bf16[1,1792,1248]{1,2,0:T(8,128)(2,1)} fusion(bf16[768,1792]{1,0:T(8,128)(2,1)} %bitcast.11, bf16[768,1248]{1,0:T(8,128)(2,1)} %bitcast.13), kind=kOutput, calls=%fused_computation.2 | convolution fusion | flops 3439607808 | bytes 9142272 | tf_op jit(solution)/shard_map/dot_general | solution.py:316
  63.5 0.0 copy-done.4
  63.5 0.0 copy-done.5
  63.5 0.0 copy-start.1
  63.6 0.0 copy-start
  63.6 0.0 copy-start.3
  63.6 0.0 copy-start.2
  63.6 2.1 %fusion.2 = bf16[1792,312]{0,1:T(8,128)(2,1)} fusion(bf16[768,1792]{1,0:T(8,128)(2,1)S(1)} %bitcast.12, bf16[768,312]{1,0:T(8,128)(2,1)S(1)} %bitcast.14), kind=kOutput, calls=%fused_computation.4 | convolution fusion | flops 859901952 | bytes 4349952 | tf_op jit(solution)/shard_map/dot_general | solution.py:319
  65.7 0.0 copy-done.1
  65.7 0.8 %copy.27 = bf16[1,156,1248]{2,1,0:T(8,128)(2,1)} copy(bf16[1,156,1248]{2,1,0:T(8,128)(2,1)S(1)} %copy-done.1) | data formatting | bytes 778752
  66.5 0.0 copy-done
  66.5 0.8 %copy.28 = bf16[1,156,1248]{2,1,0:T(8,128)(2,1)} copy(bf16[1,156,1248]{2,1,0:T(8,128)(2,1)S(1)} %copy-done) | data formatting | bytes 778752
  67.2 0.0 copy-done.3
  67.2 0.7 copy.29
  67.9 0.0 copy-done.2
  67.9 0.7 copy.30
  (1 shorter events, 0.0 us)
Async XLA Ops:
  55.2 8.3 %copy-start.4 = (bf16[4,4,48,1792]{3,2,1,0:T(8,128)(2,1)S(1)}, bf16[4,4,48,1792]{3,2,1,0:T(8,128)(2,1)}, u32[]{:S(2)}) copy-start(bf16[4,4,48,1792]{3,2,1,0:T(8,128)(2,1)} %get-tuple-element.18) | copy-start | bytes 8257540
  55.2 8.3 %copy-start.5 = (bf16[4,192,312]{2,1,0:T(8,128)(2,1)S(1)}, bf16[4,192,312]{2,1,0:T(8,128)(2,1)}, u32[]{:S(2)}) copy-start(bf16[4,192,312]{2,1,0:T(8,128)(2,1)} %get-tuple-element.22) | copy-start | bytes 1437700
  63.5 2.2 %copy-start.1 = (bf16[1,156,1248]{2,1,0:T(8,128)(2,1)S(1)}, bf16[1,156,1248]{2,1,0:T(8,128)(2,1)}, u32[]{:S(2)}) copy-start(bf16[1,156,1248]{2,1,0:T(8,128)(2,1)} %get-tuple-element.30) | copy-start | bytes 1168132
  63.6 2.9 %copy-start = (bf16[1,156,1248]{2,1,0:T(8,128)(2,1)S(1)}, bf16[1,156,1248]{2,1,0:T(8,128)(2,1)}, u32[]{:S(2)}) copy-start(bf16[1,156,1248]{2,1,0:T(8,128)(2,1)} %get-tuple-element.31) | copy-start | bytes 1168132
  63.6 3.7 %copy-start.3 = (bf16[192,312]{1,0:T(8,128)(2,1)S(1)}, bf16[192,312]{1,0:T(8,128)(2,1)}, u32[]{:S(2)}) copy-start(bf16[192,312]{1,0:T(8,128)(2,1)} %get-tuple-element.34) | copy-start | bytes 359428
  63.6 4.3 %copy-start.2 = (bf16[192,312]{1,0:T(8,128)(2,1)S(1)}, bf16[192,312]{1,0:T(8,128)(2,1)}, u32[]{:S(2)}) copy-start(bf16[192,312]{1,0:T(8,128)(2,1)} %get-tuple-element.35) | copy-start | bytes 359428

commit v3 on v2

--- a/solution.py
+++ b/solution.py
@@ -10,6 +10,7 @@
 MESH = pl.DeviceIdType.MESH
 BF = jnp.bfloat16
 F32 = jnp.float32
+VMEM_LIMIT = 52 * 2**20
 
 
 def silu_parts(gate_val):
@@ -32,9 +33,9 @@
 
 
 def layer_kernel(
-    n_dp, n_z, grad, meta_in, expert_w, dense_w, gate_pre, up_pre, dense_gate_pre, dense_up_pre,
+    n_dp, n_z, grad, ids, places, probs, expert_w, dense_w, gate_pre, up_pre, dense_gate_pre, dense_up_pre,
     slices, weighted, dh, gate_out, up_out, dgate_out, dup_out, dots_out,
-    rows, hid, meta, w, dw, acc, dacc, dots,
+    rows, hid, meta, table, w, dw, acc, dacc, dots,
     loc, w_sem, dw_sem, z_send, z_recv, sib_send, sl_send, sl_recv, slf_send,
     mz_send, mz_recv, md_send, md_recv, hid_send, hid_recv, dh_send, dh_recv,
     hf_send, hf_recv, df_send, df_recv, dot_send, dot_recv,
@@ -84,12 +85,10 @@
         return pl.ds(pl.multiple_of(j * unit, unit), unit)
 
     def local_copies():
-        out = [
+        return [
             pltpu.make_async_copy(grad.at[:, pl.ds(j * unit, unit)], rows.at[j, z], loc.at[j])
             for j in range(n_dp)
         ]
-        out.append(pltpu.make_async_copy(meta_in, meta.at[d, z], loc.at[n_dp]))
-        return out
 
     def weight_copies(j):
         return (
@@ -99,7 +98,14 @@
 
     for copy in local_copies():
         copy.start()
-
+    for j in range(n_dp):
+        for copy in weight_copies((j * half) % n_dp + (j * half) // n_dp):
+            copy.start()
+
+    table[...] = jnp.zeros(table.shape, F32)
+    for k, ref in enumerate((ids, places, probs)):
+        table[pl.ds(2 * k, 2), pl.ds(0, tok)] = ref[...].astype(F32)
+    meta[d, z] = table[...].T[:tok].astype(BF)
     hid[d] = jnp.zeros(hid.shape[1:], BF)
     activated, _ = silu_parts(gate_pre[0].astype(F32))
     hid[d, pl.ds(0, slots), :] = (activated * up_pre[0].astype(F32)).astype(BF)
@@ -108,33 +114,35 @@
 
     pl.semaphore_wait(barrier, n_dp + jnp.where(z > 0, 1, 0) + jnp.where(z < n_z - 1, 1, 0))
 
-    def spread(zb, jj, src, ok):
+    def along_z(zb, jj, src, ok):
         j = c * half + jj
         launch(ok & (zb <= z) & (z < n_z - 1), lambda: remote(
             src, rows.at[j, zb], z_send.at[0, jj, zb], z_recv.at[j, zb], (d, z + 1, c)))
         launch(ok & (zb >= z) & (z > 0), lambda: remote(
             src, rows.at[j, zb], z_send.at[1, jj, zb], z_recv.at[j, zb], (d, z - 1, c)))
+
+    def over_dp(zb, jj, src, ok):
+        j = c * half + jj
         launch(ok & (j != d), lambda: remote(
             src, slices.at[d, zb], sl_send.at[jj, zb], sl_recv.at[d, zb], (j, z, c)))
 
-    def spread_meta(zb, src, ok):
+    def spread_meta(zb, ok):
+        src = meta.at[d, zb]
         launch(ok & (zb <= z) & (z < n_z - 1), lambda: remote(
-            src, meta.at[d, zb], mz_send.at[0, zb], mz_recv.at[zb], (d, z + 1, c)))
+            src, src, mz_send.at[0, zb], mz_recv.at[zb], (d, z + 1, c)))
         launch(ok & (zb >= z) & (z > 0), lambda: remote(
-            src, meta.at[d, zb], mz_send.at[1, zb], mz_recv.at[zb], (d, z - 1, c)))
+            src, src, mz_send.at[1, zb], mz_recv.at[zb], (d, z - 1, c)))
 
     yes = z >= 0
-    spread_meta(z, meta_in, yes)
+    spread_meta(z, yes)
+    along_z(z, 0, grad.at[:, cols(c * half)], yes)
     for jj in range(half):
-        spread(z, jj, grad.at[:, cols(c * half + jj)], yes)
+        over_dp(z, jj, grad.at[:, cols(c * half + jj)], yes)
     for k, q in enumerate(peers[:2]):
         launch(True, lambda k=k, q=q: remote(
             hid.at[d], hid.at[d], hid_send.at[k], hid_recv.at[d], (q, z, c)))
         launch(True, lambda k=k, q=q: remote(
             dh.at[d], dh.at[d], dh_send.at[k], dh_recv.at[d], (q, z, c)))
-    for j in range(n_dp):
-        for copy in weight_copies(j):
-            copy.start()
 
     def arrived(dst, rsem):
         return remote(dst, dst, loc.at[0], rsem, sib)
@@ -158,54 +166,90 @@
             launch(ok & own_half, lambda q=q: remote(
                 slices.at[q, zb], slices.at[q, zb], slf_send.at[q, zb], sl_recv.at[q, zb], sib))
 
-    order = [(z + sign * dist, dist) for dist in range(1, n_z) for sign in (-1, 1)]
-    for step, (zb, dist) in enumerate(order):
-        if step == 2 * (n_z - 2):
-            pass_hidden()
-        ok = (zb >= 0) & (zb < n_z)
-        pl.when(ok)(lambda: arrived(meta.at[d, zb], mz_recv.at[zb]).wait_recv())
-        spread_meta(zb, meta.at[d, zb], ok)
-        for jj in range(half):
-            j = c * half + jj
+    def ring(dist):
+        return [(zb, (zb >= 0) & (zb < n_z)) for zb in (z - dist, z + dist)]
+
+    def relay_rows(jj, dist):
+        j = c * half + jj
+        for zb, ok in ring(dist):
             pl.when(ok)(lambda: arrived(rows.at[j, zb], z_recv.at[j, zb]).wait_recv())
-            spread(zb, jj, rows.at[j, zb], ok)
-            launch(ok, lambda zb=zb, jj=jj, j=j: remote(
+            along_z(zb, jj, rows.at[j, zb], ok)
+            launch(ok, lambda zb=zb: remote(
                 rows.at[j, zb], rows.at[j, zb], sib_send.at[jj, zb], z_recv.at[j, zb], sib))
-    for copy in local_copies():
-        copy.wait()
+            over_dp(zb, jj, rows.at[j, zb], ok)
+
+    def relay_slices(dist):
+        for zb, ok in [(z, yes)] if dist == 0 else ring(dist):
+            pass_slices(zb, ok)
+
+    for dist in range(1, n_z):
+        for zb, ok in ring(dist):
+            pl.when(ok)(lambda: arrived(meta.at[d, zb], mz_recv.at[zb]).wait_recv())
+            spread_meta(zb, ok)
     for k, q in enumerate(peers):
         launch(True, lambda k=k, q=q: remote(
             meta.at[d], meta.at[d], md_send.at[k], md_recv.at[d], (q, z, c)))
-    pass_slices(z, yes)
-    for zb, dist in order[:2]:
-        pass_slices(zb, (zb >= 0) & (zb < n_z))
-    for zb, _ in order:
-        ok = (zb >= 0) & (zb < n_z)
-        for jj in range(half):
-            j = (1 - c) * half + jj
-            pl.when(ok)(lambda: arrived(rows.at[j, zb], z_recv.at[j, zb]).wait_recv())
+
+    mine = z.astype(F32)
+
+    def place(q):
+        _, weight_q = selection(
+            meta[q].reshape(n_z * tok, meta.shape[-1]), mine, capacity, padded, tok
+        )
+        weighted[q] = jnp.dot(weight_q, hid[q], preferred_element_type=F32).astype(BF)
+
+    acc[...] = jnp.zeros_like(acc)
+    dacc[...] = jnp.zeros_like(dacc)
+    by_token = (((0,), (0,)), ((), ()))
+    by_width = (((1,), (1,)), ((), ()))
+
+    def back(jj):
+        info = meta[d].reshape(n_z * tok, meta.shape[-1])
+        pick, _ = selection(info, mine, capacity, padded, tok)
+
+        def unit_of(i, _):
+            j = jj + half * i
+            for copy in weight_copies(j):
+                copy.wait()
+            tokens = rows[j].reshape(n_z * tok, unit)
+            routed = lax.dot_general(pick, tokens, by_token, preferred_element_type=F32).astype(BF)
+            acc[...] += lax.dot_general(routed, w[j], by_width, preferred_element_type=F32)
+            dacc[...] += lax.dot_general(tokens, dw[j], by_width, preferred_element_type=F32)
+            return 0
+
+        lax.fori_loop(0, n_dp // half, unit_of, 0)
+
+    def from_sibling(jj):
+        j = (1 - c) * half + jj
+        for dist in range(1, n_z):
+            for zb, ok in ring(dist):
+                pl.when(ok)(lambda: arrived(rows.at[j, zb], z_recv.at[j, zb]).wait_recv())
+
+    for jj in range(half):
+        for dist in range(1, n_z):
+            if jj == half - 1 and dist == n_z - 1:
+                pass_hidden()
+                for q in peers:
+                    arrived(meta.at[q], md_recv.at[q]).wait_recv()
+                place(d)
+                place(flip_x)
+                place(flip_y)
+                for copy in local_copies():
+                    copy.wait()
+                for early in range(half - 1):
+                    from_sibling(early)
+                    back(early)
+                relay_slices(0)
+            relay_rows(jj, dist)
+            if dist == 1 and jj < half - 1:
+                along_z(z, jj + 1, grad.at[:, cols(c * half + jj + 1)], yes)
+    relay_slices(1)
+    from_sibling(half - 1)
     own = pltpu.make_async_copy(rows.at[d], slices.at[d], loc.at[0])
     own.start()
-
-    mine = z.astype(F32)
-    info = meta[d].reshape(n_z * tok, meta.shape[-1])
-    pick, weight = selection(info, mine, capacity, padded, tok)
-    by_token = (((0,), (0,)), ((), ()))
-    by_width = (((1,), (1,)), ((), ()))
-    acc[...] = jnp.zeros_like(acc)
-    dacc[...] = jnp.zeros_like(dacc)
-
-    def back(j, _):
-        for copy in weight_copies(j):
-            copy.wait()
-        tokens = rows[j].reshape(n_z * tok, unit)
-        routed = lax.dot_general(pick, tokens, by_token, preferred_element_type=F32).astype(BF)
-        acc[...] += lax.dot_general(routed, w[j], by_width, preferred_element_type=F32)
-        dacc[...] += lax.dot_general(tokens, dw[j], by_width, preferred_element_type=F32)
-        return 0
-
-    lax.fori_loop(0, n_dp, back, 0)
-
+    back(half - 1)
+
+    _, weight = selection(meta[d].reshape(n_z * tok, meta.shape[-1]), mine, capacity, padded, tok)
     prob = lax.dot_general(
         weight, jnp.ones((n_z * tok, 128), BF), by_token, preferred_element_type=F32
     )[:slots, 0:1]
@@ -216,8 +260,8 @@
     dots[0] = jnp.zeros(dots.shape[1:], F32)
     dots[0, pl.ds(0, slots), :] = jnp.broadcast_to(partial, (slots, 128))
     launch(True, lambda: remote(dots.at[0], dots.at[1], dot_send, dot_recv, sib))
-    for zb, dist in order[2:]:
-        pass_slices(zb, (zb >= 0) & (zb < n_z))
+    for dist in range(2, n_z):
+        relay_slices(dist)
     scaled = prob * back_hidden
     gate_out[0] = (scaled * up_val * slope).astype(BF)
     up_out[0] = (scaled * activated).astype(BF)
@@ -226,36 +270,29 @@
     dgate_out[...] = (dacc[...] * dense_up * slope).astype(BF)
     dup_out[...] = (dacc[...] * activated).astype(BF)
 
-    for q in peers:
-        arrived(meta.at[q], md_recv.at[q]).wait_recv()
     for k in range(2):
         part = pl.ds(k * (padded // 2), padded // 2)
         dpart = pl.ds(k * (dh.shape[1] // 2), dh.shape[1] // 2)
         arrived(hid.at[diag, part], hf_recv.at[k]).wait_recv()
         arrived(dh.at[diag, dpart], df_recv.at[k]).wait_recv()
-
-    def place(q, _):
-        _, weight_q = selection(
-            meta[q].reshape(n_z * tok, meta.shape[-1]), mine, capacity, padded, tok
-        )
-        weighted[q] = jnp.dot(weight_q, hid[q], preferred_element_type=F32).astype(BF)
-        return 0
-
-    lax.fori_loop(0, n_dp, place, 0)
+    place(diag)
     arrived(dots.at[1], dot_recv).wait_recv()
-    dots_out[...] = dots[0] + dots[1]
+    dots_out[...] = (dots[0] + dots[1]).T[0:1, :slots]
     own.wait()
     for cond, make in pending:
         when(cond, lambda: make().wait_send())
 
 
-def layer(grad_out, meta_in, expert_down, dense_down, gate_pre, up_pre, dense_gate, dense_up, n_dp, n_z):
+def layer(
+    grad_out, ids, places, probs, expert_down, dense_down, gate_pre, up_pre, dense_gate, dense_up, n_dp, n_z
+):
     tok, width = grad_out.shape
     unit = width // n_dp
     half = n_dp // 2
     _, slots, he = gate_pre.shape
     tokens, hd = dense_gate.shape
     padded = -(-slots // 32) * 32
+    square = -(-slots // 128) * 128
     vm = pl.BlockSpec(memory_space=pltpu.VMEM)
     hbm = pl.BlockSpec(memory_space=pl.ANY)
     dma = pltpu.SemaphoreType.DMA
@@ -270,19 +307,20 @@
             shape(gate_pre.shape, BF),
             shape(dense_gate.shape, BF),
             shape(dense_gate.shape, BF),
-            shape((padded, 128), F32),
+            shape((1, slots), F32),
         ),
-        in_specs=[hbm, vm, hbm, hbm, vm, vm, vm, vm],
+        in_specs=[hbm, vm, vm, vm, hbm, hbm, vm, vm, vm, vm],
         out_specs=(vm,) * 8,
         scratch_shapes=[
             pltpu.VMEM((n_dp, n_z, tok, unit), BF),
             pltpu.VMEM((n_dp, padded, he), BF),
-            pltpu.VMEM((n_dp, n_z) + meta_in.shape, BF),
+            pltpu.VMEM((n_dp, n_z, tok, 128), BF),
+            pltpu.VMEM((128, 128), F32),
             pltpu.VMEM((n_dp, he, unit), BF),
             pltpu.VMEM((n_dp, hd, unit), BF),
             pltpu.VMEM((padded, he), F32),
             pltpu.VMEM((tokens, hd), F32),
-            pltpu.VMEM((2, padded, 128), F32),
+            pltpu.VMEM((2, square, 128), F32),
             dma((n_dp + 1,)), dma((n_dp,)), dma((n_dp,)),
             dma((2, half, n_z)), dma((n_dp, n_z)), dma((half, n_z)),
             dma((half, n_z)), dma((n_dp, n_z)), dma((n_dp, n_z)),
@@ -291,9 +329,62 @@
             dma((2,)), dma((2,)), dma((2,)), dma((2,)), dma, dma,
         ],
         compiler_params=pltpu.CompilerParams(
-            collective_id=0, has_side_effects=True, vmem_limit_bytes=58 * 2**20
+            collective_id=0, has_side_effects=True, vmem_limit_bytes=VMEM_LIMIT
         ),
-    )(grad_out, meta_in, expert_down, dense_down, gate_pre, up_pre, dense_gate, dense_up)
+    )(grad_out, ids, places, probs, expert_down, dense_down, gate_pre, up_pre, dense_gate, dense_up)
+
+
+def final_kernel(scale, slices, weighted, dh, *refs):
+    count = (len(refs) - 3) // 2
+    given, (expert_out, dense_out), taken, sem = (
+        refs[:count], refs[count:count + 2], refs[count + 2:-1], refs[-1]
+    )
+    copies = [pltpu.make_async_copy(a, b, sem.at[i]) for i, (a, b) in enumerate(zip(given, taken))]
+    step = pl.program_id(0)
+
+    @pl.when(step == 0)
+    def _():
+        for copy in copies:
+            copy.start()
+
+    contract = (((0,), (0,)), ((), ()))
+    right = slices[...]
+    expert_out[0] = (
+        lax.dot_general(weighted[...], right, contract, preferred_element_type=F32) * scale
+    ).astype(BF)
+    dense_out[...] = (
+        lax.dot_general(dh[...], right, contract, preferred_element_type=F32) * scale
+    ).astype(BF)
+
+    @pl.when(step == pl.num_programs(0) - 1)
+    def _():
+        for copy in copies:
+            copy.wait()
+
+
+def final(slices, weighted, dh, small, scale):
+    tokens, unit = slices.shape
+    he, hd = weighted.shape[1], dh.shape[1]
+    tile = unit // 2 if unit % 256 == 0 else unit
+    hbm = pl.BlockSpec(memory_space=pl.ANY)
+    shape = jax.ShapeDtypeStruct
+    return pl.pallas_call(
+        functools.partial(final_kernel, scale),
+        grid=(unit // tile,),
+        out_shape=(shape((1, he, unit), BF), shape((hd, unit), BF))
+        + tuple(shape(a.shape, a.dtype) for a in small),
+        in_specs=[
+            pl.BlockSpec((tokens, tile), lambda i: (0, i)),
+            pl.BlockSpec((tokens, he), lambda i: (0, 0)),
+            pl.BlockSpec((tokens, hd), lambda i: (0, 0)),
+        ] + [hbm] * len(small),
+        out_specs=(
+            pl.BlockSpec((1, he, tile), lambda i: (0, 0, i)),
+            pl.BlockSpec((hd, tile), lambda i: (0, i)),
+        ) + (hbm,) * len(small),
+        scratch_shapes=[pltpu.SemaphoreType.DMA((len(small),))],
+        compiler_params=pltpu.CompilerParams(vmem_limit_bytes=32 * 2**20),
+    )(slices, weighted, dh, *small)
 
 
 def local_fast(
@@ -302,32 +393,15 @@
 ):
     n_z = lax.axis_size("expert")
     n_dp = lax.axis_size("dp")
-    tok = grad_out.shape[0]
-    slots = expert_gate_pre.shape[1]
-    meta_in = jnp.concatenate(
-        [expert_ids.astype(BF), slot_positions.astype(BF), gate_prob, jnp.zeros((tok, 122), BF)], axis=1
-    )
-    slices, weighted, dh, gate_grad, up_grad, dgate_grad, dup_grad, dots = layer(
-        grad_out, meta_in, expert_down, dense_down,
+    slices, weighted, dh, *small = layer(
+        grad_out, expert_ids.T, slot_positions.T, gate_prob.T, expert_down, dense_down,
         expert_gate_pre, expert_up_pre, dense_gate_pre, dense_up_pre, n_dp, n_z,
     )
-    every = slices.reshape(-1, slices.shape[-1])
-    contract = (((0,), (0,)), ((), ()))
-    expert_sum = lax.dot_general(
-        every, weighted.reshape(every.shape[0], -1), contract, preferred_element_type=F32
-    )
-    dense_sum = lax.dot_general(
-        every, dh.reshape(every.shape[0], -1), contract, preferred_element_type=F32
-    )
-    return (
-        gate_grad,
-        up_grad,
-        dots[:slots, 0][None],
-        (expert_sum / n_dp).astype(BF)[None],
-        dgate_grad,
-        dup_grad,
-        (dense_sum / n_dp).astype(BF),
-    )
+    tokens = slices.shape[0] * slices.shape[1] * slices.shape[2]
+    expert_grad, dense_grad, gate_grad, up_grad, dgate_grad, dup_grad, dots = final(
+        slices.reshape(tokens, -1), weighted.reshape(tokens, -1), dh.reshape(tokens, -1), small, 1.0 / n_dp
+    )
+    return (gate_grad, up_grad, dots, expert_grad.transpose(0, 2, 1), dgate_grad, dup_grad, dense_grad.T)
 
 
 def local_plain(

time: 68.8 us -> 67.3 us (0.978)
  the two profiles are of different devices: /device:TPU:11 before, /device:TPU:1 now
where the time goes in v3:
time: 67.3 us; the launch traced here: 66.7 us
  Pallas kernels  56.9 us (85%)
  local copies, waits for them, and re-layouts  9.2 us (14%)
    pallas_call x1, Pallas kernels, layer(): pl.pallas_call(functools.partial(layer_kernel, n_dp, n_z), out_shape=(sha...  49.6 us
    unnamed x18, local copies, waits for them, and re-layouts  9.2 us
    pallas_call x1, Pallas kernels, final(): pl.pallas_call(functools.partial(final_kernel, scale), grid=(unit // tile...  7.26 us

profile of v3, /device:TPU:1, one launch (start us, length us, event | category | flops | bytes accessed | tf_op | source)
XLA Modules:
  0.0 66.7 jit_solution(3884821023113116305)
XLA Ops:
  0.6 0.0 copy-start.3
  0.6 1.0 %copy-done.3 = bf16[1,156,1248]{2,1,0:T(8,128)(2,1)S(1)} copy-done((bf16[1,156,1248]{2,1,0:T(8,128)(2,1)S(1)}, bf16[1,156,1248]{2,1,0:T(8,128)(2,1)}, u32[]{:S(2)}) %copy-start.3) | copy-done | bytes 389400
  1.6 0.0 copy-start.4
  1.6 0.9 %copy-done.4 = bf16[192,312]{1,0:T(8,128)(2,1)S(1)} copy-done((bf16[192,312]{1,0:T(8,128)(2,1)S(1)}, bf16[192,312]{1,0:T(8,128)(2,1)}, u32[]{:S(2)}) %copy-start.4) | copy-done | bytes 119832
  2.5 0.0 copy-start.5
  2.6 0.9 %copy-done.5 = bf16[192,312]{1,0:T(8,128)(2,1)S(1)} copy-done((bf16[192,312]{1,0:T(8,128)(2,1)S(1)}, bf16[192,312]{1,0:T(8,128)(2,1)}, u32[]{:S(2)}) %copy-start.5) | copy-done | bytes 119832
  3.5 0.0 copy-start.6
  3.5 0.7 %copy-done.6 = s32[48,2]{0,1:T(2,128)S(1)} copy-done((s32[48,2]{0,1:T(2,128)S(1)}, s32[48,2]{0,1:T(2,128)}, u32[]{:S(2)}) %copy-start.6) | copy-done | bytes 408
  4.1 0.0 copy-start.7
  4.1 0.7 %copy-done.7 = s32[48,2]{0,1:T(2,128)S(1)} copy-done((s32[48,2]{0,1:T(2,128)S(1)}, s32[48,2]{0,1:T(2,128)}, u32[]{:S(2)}) %copy-start.7) | copy-done | bytes 408
  4.8 0.0 copy-start.8
  4.8 0.7 copy-done.8
  5.5 49.6 %shard_map.153 = (bf16[4,4,48,1792]{3,2,1,0:T(8,128)(2,1)}, bf16[4,192,1248]{2,1,0:T(8,128)(2,1)}, bf16[4,192,312]{2,1,0:T(8,128)(2,1)}, bf16[1,156,1248]{2,1,0:...) custom-call(bf16[48,7168]{1,0:T(8,128)(2,1)} %grad.1, ...), custom_call_target="tpu_custom_call" | custom-call | tf_op jit(solution)/shard_map/pallas_call | solution.py:300
  55.1 0.0 copy-start
  55.1 1.8 %copy-done = bf16[4,4,48,1792]{3,2,1,0:T(8,128)(2,1)S(1)} copy-done((bf16[4,4,48,1792]{3,2,1,0:T(8,128)(2,1)S(1)}, bf16[4,4,48,1792]{3,2,1,0:T(8,128)(2,1)}, u32[]{:S(2)}) %copy-start) | copy-done | bytes 2752536
  56.9 0.0 copy-start.1
  56.9 1.5 %copy-done.1 = bf16[4,192,1248]{2,1,0:T(8,128)(2,1)S(1)} copy-done((bf16[4,192,1248]{2,1,0:T(8,128)(2,1)S(1)}, bf16[4,192,1248]{2,1,0:T(8,128)(2,1)}, u32[]{:S(2)}) %copy-start.1) | copy-done | bytes 1916952
  58.4 0.0 copy-start.2
  58.4 1.1 %copy-done.2 = bf16[4,192,312]{2,1,0:T(8,128)(2,1)S(1)} copy-done((bf16[4,192,312]{2,1,0:T(8,128)(2,1)S(1)}, bf16[4,192,312]{2,1,0:T(8,128)(2,1)}, u32[]{:S(2)}) %copy-start.2) | copy-done | bytes 479256
  59.5 7.3 %shard_map.154 = (bf16[1,1248,1792]{2,1,0:T(8,128)(2,1)}, bf16[312,1792]{1,0:T(8,128)(2,1)}, bf16[1,156,1248]{2,1,0:T(8,128)(2,1)}, bf16[1,156,1248]{2,1,0:T(8,1...) custom-call(bf16[768,1792]{1,0:T(8,128)(2,1)S(1)} %bitcast.8, ...), custom_call_target="tpu_custom_call" | custom-call | tf_op jit(solution)/shard_map/pallas_call | solution.py:371
Async XLA Ops:
  0.6 1.0 %copy-start.3 = (bf16[1,156,1248]{2,1,0:T(8,128)(2,1)S(1)}, bf16[1,156,1248]{2,1,0:T(8,128)(2,1)}, u32[]{:S(2)}) copy-start(bf16[1,156,1248]{2,1,0:T(8,128)(2,1)} %gate_pre.1) | copy-start | bytes 1168132
  1.6 0.9 %copy-start.4 = (bf16[192,312]{1,0:T(8,128)(2,1)S(1)}, bf16[192,312]{1,0:T(8,128)(2,1)}, u32[]{:S(2)}) copy-start(bf16[192,312]{1,0:T(8,128)(2,1)} %dense_gate_pre.1) | copy-start | bytes 359428
  2.5 0.9 %copy-start.5 = (bf16[192,312]{1,0:T(8,128)(2,1)S(1)}, bf16[192,312]{1,0:T(8,128)(2,1)}, u32[]{:S(2)}) copy-start(bf16[192,312]{1,0:T(8,128)(2,1)} %dense_up_pre.1) | copy-start | bytes 359428
  3.5 0.7 %copy-start.6 = (s32[48,2]{0,1:T(2,128)S(1)}, s32[48,2]{0,1:T(2,128)}, u32[]{:S(2)}) copy-start(s32[48,2]{0,1:T(2,128)} %param.12) | copy-start | bytes 1156
  4.1 0.7 %copy-start.7 = (s32[48,2]{0,1:T(2,128)S(1)}, s32[48,2]{0,1:T(2,128)}, u32[]{:S(2)}) copy-start(s32[48,2]{0,1:T(2,128)} %param.13) | copy-start | bytes 1156
  4.8 0.7 copy-start.8
  55.1 1.8 %copy-start = (bf16[4,4,48,1792]{3,2,1,0:T(8,128)(2,1)S(1)}, bf16[4,4,48,1792]{3,2,1,0:T(8,128)(2,1)}, u32[]{:S(2)}) copy-start(bf16[4,4,48,1792]{3,2,1,0:T(8,128)(2,1)} %get-tuple-element.22) | copy-start | bytes 8257540
  56.9 1.5 %copy-start.1 = (bf16[4,192,1248]{2,1,0:T(8,128)(2,1)S(1)}, bf16[4,192,1248]{2,1,0:T(8,128)(2,1)}, u32[]{:S(2)}) copy-start(bf16[4,192,1248]{2,1,0:T(8,128)(2,1)} %get-tuple-element.23) | copy-start | bytes 5750788
  58.4 1.1 %copy-start.2 = (bf16[4,192,312]{2,1,0:T(8,128)(2,1)S(1)}, bf16[4,192,312]{2,1,0:T(8,128)(2,1)}, u32[]{:S(2)}) copy-start(bf16[4,192,312]{2,1,0:T(8,128)(2,1)} %get-tuple-element.24) | copy-start | bytes 1437700

commit v4 on v3

--- a/solution.py
+++ b/solution.py
@@ -10,7 +10,7 @@
 MESH = pl.DeviceIdType.MESH
 BF = jnp.bfloat16
 F32 = jnp.float32
-VMEM_LIMIT = 52 * 2**20
+VMEM_LIMIT = 60 * 2**20
 
 
 def silu_parts(gate_val):
@@ -38,7 +38,7 @@
     rows, hid, meta, table, w, dw, acc, dacc, dots,
     loc, w_sem, dw_sem, z_send, z_recv, sib_send, sl_send, sl_recv, slf_send,
     mz_send, mz_recv, md_send, md_recv, hid_send, hid_recv, dh_send, dh_recv,
-    hf_send, hf_recv, df_send, df_recv, dot_send, dot_recv,
+    hf_send, hf_recv, df_send, df_recv, dot_send, dot_recv, slz_send,
 ):
     d, z, c = lax.axis_index("dp"), lax.axis_index("expert"), lax.axis_index("tensor")
     half = n_dp // 2
@@ -160,11 +160,15 @@
 
     own_half = c == d // half
 
-    def pass_slices(zb, ok):
+    def pass_slices(zb, ok, own=False):
         for q in peers:
             pl.when(ok)(lambda: arrived(slices.at[q, zb], sl_recv.at[q, zb]).wait_recv())
             launch(ok & own_half, lambda q=q: remote(
                 slices.at[q, zb], slices.at[q, zb], slf_send.at[q, zb], sl_recv.at[q, zb], sib))
+            for k, (step, there) in enumerate(((1, z < n_z - 1), (-1, z > 0)) if own else ()):
+                launch(own_half & there, lambda q=q, k=k, step=step: remote(
+                    slices.at[q, zb], slices.at[q, zb], slz_send.at[k, q], sl_recv.at[q, zb],
+                    (d, z + step, c)))
 
     def ring(dist):
         return [(zb, (zb >= 0) & (zb < n_z)) for zb in (z - dist, z + dist)]
@@ -176,11 +180,12 @@
             along_z(zb, jj, rows.at[j, zb], ok)
             launch(ok, lambda zb=zb: remote(
                 rows.at[j, zb], rows.at[j, zb], sib_send.at[jj, zb], z_recv.at[j, zb], sib))
-            over_dp(zb, jj, rows.at[j, zb], ok)
+            if dist > 1:
+                over_dp(zb, jj, rows.at[j, zb], ok)
 
     def relay_slices(dist):
         for zb, ok in [(z, yes)] if dist == 0 else ring(dist):
-            pass_slices(zb, ok)
+            pass_slices(zb, ok, dist == 0)
 
     for dist in range(1, n_z):
         for zb, ok in ring(dist):
@@ -227,8 +232,10 @@
 
     for jj in range(half):
         for dist in range(1, n_z):
+            if jj == half - 1 and dist == n_z - 2:
+                pass_hidden()
             if jj == half - 1 and dist == n_z - 1:
-                pass_hidden()
+                relay_slices(0)
                 for q in peers:
                     arrived(meta.at[q], md_recv.at[q]).wait_recv()
                 place(d)
@@ -239,11 +246,9 @@
                 for early in range(half - 1):
                     from_sibling(early)
                     back(early)
-                relay_slices(0)
             relay_rows(jj, dist)
             if dist == 1 and jj < half - 1:
                 along_z(z, jj + 1, grad.at[:, cols(c * half + jj + 1)], yes)
-    relay_slices(1)
     from_sibling(half - 1)
     own = pltpu.make_async_copy(rows.at[d], slices.at[d], loc.at[0])
     own.start()
@@ -260,8 +265,6 @@
     dots[0] = jnp.zeros(dots.shape[1:], F32)
     dots[0, pl.ds(0, slots), :] = jnp.broadcast_to(partial, (slots, 128))
     launch(True, lambda: remote(dots.at[0], dots.at[1], dot_send, dot_recv, sib))
-    for dist in range(2, n_z):
-        relay_slices(dist)
     scaled = prob * back_hidden
     gate_out[0] = (scaled * up_val * slope).astype(BF)
     up_out[0] = (scaled * activated).astype(BF)
@@ -276,6 +279,8 @@
         arrived(hid.at[diag, part], hf_recv.at[k]).wait_recv()
         arrived(dh.at[diag, dpart], df_recv.at[k]).wait_recv()
     place(diag)
+    for dist in range(1, n_z):
+        relay_slices(dist)
     arrived(dots.at[1], dot_recv).wait_recv()
     dots_out[...] = (dots[0] + dots[1]).T[0:1, :slots]
     own.wait()
@@ -326,7 +331,7 @@
             dma((half, n_z)), dma((n_dp, n_z)), dma((n_dp, n_z)),
             dma((2, n_z)), dma((n_z,)), dma((n_dp,)), dma((n_dp,)),
             dma((2,)), dma((n_dp,)), dma((2,)), dma((n_dp,)),
-            dma((2,)), dma((2,)), dma((2,)), dma((2,)), dma, dma,
+            dma((2,)), dma((2,)), dma((2,)), dma((2,)), dma, dma, dma((2, n_dp)),
         ],
         compiler_params=pltpu.CompilerParams(
             collective_id=0, has_side_effects=True, vmem_limit_bytes=VMEM_LIMIT
@@ -383,7 +388,7 @@
             pl.BlockSpec((hd, tile), lambda i: (0, i)),
         ) + (hbm,) * len(small),
         scratch_shapes=[pltpu.SemaphoreType.DMA((len(small),))],
-        compiler_params=pltpu.CompilerParams(vmem_limit_bytes=32 * 2**20),
+        compiler_params=pltpu.CompilerParams(vmem_limit_bytes=VMEM_LIMIT),
     )(slices, weighted, dh, *small)
 
 

time: 67.3 us -> 90.5 us (1.34)
  Pallas kernels: 56.9 us -> 89.7 us
  local copies, waits for them, and re-layouts: 9.2 us -> 0 us
    pallas_call x1, Pallas kernels: 7.26 us -> 38.6 us  [final(): pl.pallas_call(functools.partial(final_kernel, scale), grid=(unit // tile...]
    unnamed x18 -> x0, local copies, waits for them, and re-layouts: 9.2 us -> none
    pallas_call x1, Pallas kernels: 49.6 us -> 51.2 us  [layer(): pl.pallas_call(functools.partial(layer_kernel, n_dp, n_z), out_shape=(sha...]
where the time goes in v4:
time: 90.5 us; the launch traced here: 90.4 us
  Pallas kernels  89.7 us (99%)
    pallas_call x1, Pallas kernels, layer(): pl.pallas_call(functools.partial(layer_kernel, n_dp, n_z), out_shape=(sha...  51.2 us
    pallas_call x1, Pallas kernels, final(): pl.pallas_call(functools.partial(final_kernel, scale), grid=(unit // tile...  38.6 us

profile of v4, /device:TPU:1, one launch (start us, length us, event | category | flops | bytes accessed | tf_op | source)
XLA Modules:
  0.0 90.4 jit_solution(4343215126897937202)
XLA Ops:
  0.6 51.2 %shard_map.153 = (bf16[4,4,48,1792]{3,2,1,0:T(8,128)(2,1)}, bf16[4,192,1248]{2,1,0:T(8,128)(2,1)}, bf16[4,192,312]{2,1,0:T(8,128)(2,1)}, bf16[1,156,1248]{2,1,0:...) custom-call(bf16[48,7168]{1,0:T(8,128)(2,1)} %grad.1, ...), custom_call_target="tpu_custom_call" | custom-call | tf_op jit(solution)/shard_map/pallas_call | solution.py:305
  51.8 38.6 %shard_map.154 = (bf16[1,1248,1792]{2,1,0:T(8,128)(2,1)}, bf16[312,1792]{1,0:T(8,128)(2,1)}, bf16[1,156,1248]{2,1,0:T(8,128)(2,1)}, bf16[1,156,1248]{2,1,0:T(8,1...) custom-call(bf16[768,1792]{1,0:T(8,128)(2,1)} %bitcast.8, ...), custom_call_target="tpu_custom_call" | custom-call | tf_op jit(solution)/shard_map/pallas_call | solution.py:376

commit v5 on v4

--- a/solution.py
+++ b/solution.py
@@ -98,20 +98,10 @@
 
     for copy in local_copies():
         copy.start()
-    for j in range(n_dp):
-        for copy in weight_copies((j * half) % n_dp + (j * half) // n_dp):
-            copy.start()
-
     table[...] = jnp.zeros(table.shape, F32)
     for k, ref in enumerate((ids, places, probs)):
         table[pl.ds(2 * k, 2), pl.ds(0, tok)] = ref[...].astype(F32)
     meta[d, z] = table[...].T[:tok].astype(BF)
-    hid[d] = jnp.zeros(hid.shape[1:], BF)
-    activated, _ = silu_parts(gate_pre[0].astype(F32))
-    hid[d, pl.ds(0, slots), :] = (activated * up_pre[0].astype(F32)).astype(BF)
-    activated, _ = silu_parts(dense_gate_pre[...].astype(F32))
-    dh[d] = (activated * dense_up_pre[...].astype(F32)).astype(BF)
-
     pl.semaphore_wait(barrier, n_dp + jnp.where(z > 0, 1, 0) + jnp.where(z < n_z - 1, 1, 0))
 
     def along_z(zb, jj, src, ok):
@@ -138,6 +128,12 @@
     along_z(z, 0, grad.at[:, cols(c * half)], yes)
     for jj in range(half):
         over_dp(z, jj, grad.at[:, cols(c * half + jj)], yes)
+
+    hid[d] = jnp.zeros(hid.shape[1:], BF)
+    activated, _ = silu_parts(gate_pre[0].astype(F32))
+    hid[d, pl.ds(0, slots), :] = (activated * up_pre[0].astype(F32)).astype(BF)
+    activated, _ = silu_parts(dense_gate_pre[...].astype(F32))
+    dh[d] = (activated * dense_up_pre[...].astype(F32)).astype(BF)
     for k, q in enumerate(peers[:2]):
         launch(True, lambda k=k, q=q: remote(
             hid.at[d], hid.at[d], hid_send.at[k], hid_recv.at[d], (q, z, c)))
@@ -169,6 +165,13 @@
                 launch(own_half & there, lambda q=q, k=k, step=step: remote(
                     slices.at[q, zb], slices.at[q, zb], slz_send.at[k, q], sl_recv.at[q, zb],
                     (d, z + step, c)))
+
+    def fetch_weights(jj):
+        for i in range(n_dp // half):
+            for copy in weight_copies(jj + half * i):
+                copy.start()
+
+    fetch_weights(0)
 
     def ring(dist):
         return [(zb, (zb >= 0) & (zb < n_z)) for zb in (z - dist, z + dist)]
@@ -247,6 +250,8 @@
                     from_sibling(early)
                     back(early)
             relay_rows(jj, dist)
+            if dist == 2 and jj < half - 1:
+                fetch_weights(jj + 1)
             if dist == 1 and jj < half - 1:
                 along_z(z, jj + 1, grad.at[:, cols(c * half + jj + 1)], yes)
     from_sibling(half - 1)
@@ -340,17 +345,13 @@
 
 
 def final_kernel(scale, slices, weighted, dh, *refs):
-    count = (len(refs) - 3) // 2
-    given, (expert_out, dense_out), taken, sem = (
-        refs[:count], refs[count:count + 2], refs[count + 2:-1], refs[-1]
-    )
-    copies = [pltpu.make_async_copy(a, b, sem.at[i]) for i, (a, b) in enumerate(zip(given, taken))]
-    step = pl.program_id(0)
-
-    @pl.when(step == 0)
+    count = (len(refs) - 2) // 2
+    given, (expert_out, dense_out), taken = refs[:count], refs[count:count + 2], refs[count + 2:]
+
+    @pl.when(pl.program_id(0) == 0)
     def _():
-        for copy in copies:
-            copy.start()
+        for a, b in zip(given, taken):
+            b[...] = a[...]
 
     contract = (((0,), (0,)), ((), ()))
     right = slices[...]
@@ -361,18 +362,13 @@
         lax.dot_general(dh[...], right, contract, preferred_element_type=F32) * scale
     ).astype(BF)
 
-    @pl.when(step == pl.num_programs(0) - 1)
-    def _():
-        for copy in copies:
-            copy.wait()
-
 
 def final(slices, weighted, dh, small, scale):
     tokens, unit = slices.shape
     he, hd = weighted.shape[1], dh.shape[1]
     tile = unit // 2 if unit % 256 == 0 else unit
-    hbm = pl.BlockSpec(memory_space=pl.ANY)
     shape = jax.ShapeDtypeStruct
+    whole = [pl.BlockSpec(a.shape, lambda i, n=a.ndim: (0,) * n) for a in small]
     return pl.pallas_call(
         functools.partial(final_kernel, scale),
         grid=(unit // tile,),
@@ -382,12 +378,11 @@
             pl.BlockSpec((tokens, tile), lambda i: (0, i)),
             pl.BlockSpec((tokens, he), lambda i: (0, 0)),
             pl.BlockSpec((tokens, hd), lambda i: (0, 0)),
-        ] + [hbm] * len(small),
+        ] + whole,
         out_specs=(
             pl.BlockSpec((1, he, tile), lambda i: (0, 0, i)),
             pl.BlockSpec((hd, tile), lambda i: (0, i)),
-        ) + (hbm,) * len(small),
-        scratch_shapes=[pltpu.SemaphoreType.DMA((len(small),))],
+        ) + tuple(whole),
         compiler_params=pltpu.CompilerParams(vmem_limit_bytes=VMEM_LIMIT),
     )(slices, weighted, dh, *small)
 

time: 90.5 us -> 61.5 us (0.68)
  Pallas kernels: 89.7 us -> 60.7 us
    pallas_call x1, Pallas kernels: 38.6 us -> 9.52 us  [final(): pl.pallas_call(functools.partial(final_kernel, scale), grid=(unit // tile...]
where the time goes in v5:
time: 61.5 us; the launch traced here: 61.3 us
  Pallas kernels  60.7 us (99%)
  between operations  0.64 us (1%)
    pallas_call x1, Pallas kernels, layer(): pl.pallas_call(functools.partial(layer_kernel, n_dp, n_z), out_shape=(sha...  51.2 us
    pallas_call x1, Pallas kernels, final(): pl.pallas_call(functools.partial(final_kernel, scale), grid=(unit // tile...  9.52 us

profile of v5, /device:TPU:1, one launch (start us, length us, event | category | flops | bytes accessed | tf_op | source)
XLA Modules:
  0.0 61.3 jit_solution(17531927747022585967)
XLA Ops:
  0.6 51.2 %shard_map.153 = (bf16[4,4,48,1792]{3,2,1,0:T(8,128)(2,1)}, bf16[4,192,1248]{2,1,0:T(8,128)(2,1)}, bf16[4,192,312]{2,1,0:T(8,128)(2,1)}, bf16[1,156,1248]{2,1,0:...) custom-call(bf16[48,7168]{1,0:T(8,128)(2,1)} %grad.1, ...), custom_call_target="tpu_custom_call" | custom-call | tf_op jit(solution)/shard_map/pallas_call | solution.py:310
  51.8 9.5 %shard_map.154 = (bf16[1,1248,1792]{2,1,0:T(8,128)(2,1)}, bf16[312,1792]{1,0:T(8,128)(2,1)}, bf16[1,156,1248]{2,1,0:T(8,128)(2,1)}, bf16[1,156,1248]{2,1,0:T(8,1...) custom-call(bf16[768,1792]{1,0:T(8,128)(2,1)} %bitcast.8, ...), custom_call_target="tpu_custom_call" | custom-call | tf_op jit(solution)/shard_map/pallas_call | solution.py:372
